TPU v7x, 256 devices: a whole 4x4x8 slice. The times are simulated.
256 devices in a mesh: morton: 256 (over y, z, x, core).
Axes of the slice: x: 4, y: 4, z: 8, core: 2. Of those that a mesh axis runs over, the one named last changes fastest.
Arguments:
- offsets: float32 [3, 2097152], P(None, 'morton'), may hold values from -0.5 to 0.5
- forces: float32 [3, 2097152], P(None, 'morton'), may hold values from -6 to 6
- counts: int32 [16384], P('morton'), may hold values from 1 to 128
- uc2ue: float32 [456, 456], replicated, may hold values from -0.25 to 0.25
- m2m_ops: float32 [8, 456, 456], replicated, may hold values from -0.09375 to 0.09375
- compress: float32 [456, 64], replicated, may hold values from -0.25 to 0.25
- m2l_ops: bfloat16 [316, 64, 64], replicated, may hold values from -0.0546875 to 0.0546875
- root_ops: bfloat16 [63, 64, 64], replicated, may hold values from -0.125 to 0.125
Outputs:
- local_boxes: float32 [18688, 64], P('morton')
- local_roots: float32 [32, 64], replicated
Inputs may be any that keep to these rules, and one draw needn't show every extreme that they name: The live points of a leaf are its first counts slots; later slots belong to no point.
All inputs are finite; a program needn't handle non-finite values.
Results may differ from a plain program's by a relative error of at most 0.0031.
Values may be sent and summed in bfloat16 or wider, within the bound.
No kernel may reach another device: no remote copies, remote signals or barrier semaphores. Data moves between devices by JAX's collectives and lax.ppermute only.
A program may use at most 192 MiB of HBM per device.

v0:
```python
import functools

import jax
import jax.numpy as jnp
import ml_dtypes
import numpy as np
from jax import lax
from jax.experimental import pallas as pl
from jax.experimental.pallas import tpu as pltpu
from jax.sharding import PartitionSpec as P

SURF_ORDER = 6
NQ = 152
NCOEF = 456
RANK = 64
P_CAP = 128
LEAF_DEV = 64
BOX_DEV = 73
NROOT = 32
AXIS = "morton"
CHECK_RADIUS = 1.475
LEAF_UNROLL = 4

F32 = jnp.float32
BF16 = jnp.bfloat16


def surface_points():
    ticks = np.linspace(-1.0, 1.0, SURF_ORDER)
    last = SURF_ORDER - 1
    chosen = []
    for i in range(SURF_ORDER):
        for j in range(SURF_ORDER):
            for k in range(SURF_ORDER):
                if min(i, j, k) == 0 or max(i, j, k) == last:
                    chosen.append((ticks[i], ticks[j], ticks[k]))
    return CHECK_RADIUS * np.array(chosen).T


def direction_index():
    found = {}
    for u in range(-3, 4):
        for v in range(-3, 4):
            for w in range(-3, 4):
                if max(abs(u), abs(v), abs(w)) >= 2:
                    found[(u, v, w)] = len(found)
    return found


DIRS = direction_index()


def leaf_order():
    table = np.zeros((64, 64), np.float32)
    for leaf in range(64):
        x, y, z = leaf // 16, leaf // 4 % 4, leaf % 4
        octant = (x % 2) * 4 + (y % 2) * 2 + z % 2
        parent = (x // 2) * 4 + (y // 2) * 2 + z // 2
        table[leaf, octant * 8 + parent] = 1.0
    return table.astype(ml_dtypes.bfloat16)


def reachable(shift, target):
    return not (shift == -3 and target % 2 == 0) and not (shift == 3 and target % 2 == 1)


def cross_section_picks():
    table = np.zeros((4, 49 * 32, 128), np.float32)
    for place in range(4):
        y_bit, z_bit = place // 2, place % 2
        for pair in range(49):
            v, w = pair // 7 - 3, pair % 7 - 3
            for side, first, copies in ((4, 0, 1), (2, 16, 2)):
                for y in range(side):
                    for z in range(side):
                        if not (reachable(v, y) and reachable(w, z)):
                            continue
                        gy, gz = side * y_bit + y + v, side * z_bit + z + w
                        if not (0 <= gy < 2 * side and 0 <= gz < 2 * side):
                            continue
                        owner = (gy // side) * 2 + gz // side
                        source = (owner ^ place) * 32 + first + (gy % side) * side + gz % side
                        for copy in range(copies):
                            table[place, pair * 32 + first + 4 * copy + y * side + z, source] = 1.0
    return table.astype(ml_dtypes.bfloat16)


def device_level_table():
    rows = np.zeros((8, 24), np.int32)
    for place in range(8):
        parity, y_bit, z_bit = place // 4, place // 2 % 2, place % 2
        columns = (-2, 2, 3) if parity == 0 else (-2, -1, 3)
        for n, column in enumerate(columns):
            for other in range(4):
                entry = (column - parity, other // 2 - y_bit, other % 2 - z_bit)
                rows[place, n * 4 + other] = DIRS[entry]
            rows[place, 12 + n] = column
    return rows


def split(x):
    high = x.astype(BF16).astype(F32)
    return high, x - high


def stacked(x):
    high, low = split(x)
    return jnp.concatenate([high, low], axis=0).astype(BF16)


def dot(a, b):
    return jnp.dot(a, b, preferred_element_type=F32)


def product(x, w_high, w_low):
    rows = x.shape[0]
    both = stacked(x)
    top = dot(both, w_high)
    rest = dot(both, w_low)
    return top[:rows] + (top[rows:] + rest[:rows])


def upward_kernel(
    offsets, forces, counts, surface, order, uc2ue, m2m_hbm, compress, shared, block,
    m2m, m2m_high, m2m_low, check, sem,
):
    fetch = pltpu.make_async_copy(m2m_hbm, m2m, sem)
    fetch.start()
    slots = lax.broadcasted_iota(jnp.int32, (1, P_CAP), 1)
    zero = jnp.zeros((1, P_CAP), F32)
    one = jnp.ones((1, P_CAP), F32)

    def leaf(l, carry):
        columns = pl.ds(pl.multiple_of(l * P_CAP, P_CAP), P_CAP)
        u = offsets[:, columns]
        live = (slots < counts[l]).astype(F32)
        f = forces[:, columns] * live
        r = [surface[s] - u[s : s + 1] for s in range(3)]
        inverse = lax.rsqrt(r[0] * r[0] + r[1] * r[1] + r[2] * r[2])
        along = r[0] * f[0:1] + r[1] * f[1:2] + r[2] * f[2:3]
        pulled = along * (inverse * inverse * inverse)
        both = jnp.concatenate([inverse, pulled], axis=1)
        high, low = split(both)
        left = jnp.concatenate(
            [jnp.concatenate([f, zero], axis=0), jnp.concatenate([-u, one], axis=0)], axis=1
        )
        left = stacked(left)
        nt = (((1,), (1,)), ((), ()))
        top = lax.dot_general(left, high.astype(BF16), nt, preferred_element_type=F32)
        rest = lax.dot_general(left, low.astype(BF16), nt, preferred_element_type=F32)
        sums = top[0:4] + (top[4:8] + rest[0:4])
        octant = (l >> 4 & 1) * 4 + (l >> 2 & 1) * 2 + (l & 1)
        parent = (l >> 5 & 1) * 4 + (l >> 3 & 1) * 2 + (l >> 1 & 1)
        check[pl.ds(octant * 8 + parent, 1)] = sums[None]
        return carry

    lax.fori_loop(0, LEAF_DEV, leaf, 0, unroll=LEAF_UNROLL)

    points = surface[3][:, :]
    density = jnp.zeros((LEAF_DEV, NCOEF), F32)
    for s in range(3):
        rows = check[:, s, :] + check[:, 3, :] * points[s : s + 1, :]
        w_high, w_low = split(uc2ue[s * NQ : (s + 1) * NQ, :])
        density = density + product(rows, w_high.astype(BF16), w_low.astype(BF16))
    shrink = compress[...]
    shrink = jnp.concatenate([shrink, shrink], axis=1)
    s_high, s_low = split(shrink)
    s_high, s_low = s_high.astype(BF16), s_low.astype(BF16)
    lower = lax.broadcasted_iota(jnp.int32, (1, 128), 1) < RANK
    leaves = product(density, s_high, s_low).astype(BF16)
    leaves = dot(order[...], leaves)
    block[0:16, 0:128] = jnp.where(lower, leaves[0:16], leaves[16:32]).astype(BF16)
    block[0:16, 128:256] = jnp.where(lower, leaves[32:48], leaves[48:64]).astype(BF16)

    fetch.wait()
    parents = jnp.zeros((8, NCOEF), F32)
    for o in range(8):
        w_high, w_low = split(m2m[o])
        w_high, w_low = w_high.astype(BF16), w_low.astype(BF16)
        m2m_high[o] = w_high
        m2m_low[o] = w_low
        parents = parents + product(density[o * 8 : o * 8 + 8], w_high, w_low)
    middle = product(parents, s_high, s_low).astype(BF16).astype(F32)
    middle = jnp.where(lower, middle[0:4], middle[4:8])

    def one_row(x, w_high, w_low):
        high, low = split(x)
        row = lax.broadcasted_iota(jnp.int32, (8, 1), 0)
        both = jnp.where(row == 0, high, jnp.where(row == 1, low, 0.0)).astype(BF16)
        top = dot(both, w_high)
        rest = dot(both, w_low)
        return top[0:1] + (top[1:2] + rest[0:1])

    device = jnp.zeros((1, NCOEF), F32)
    for o in range(8):
        device = device + one_row(parents[o : o + 1], m2m_high[o], m2m_low[o])
    own = one_row(device, s_high, s_low).astype(BF16).astype(F32)
    octant = lax.axis_index(AXIS) % 8
    above = one_row(device, m2m_high[octant], m2m_low[octant])
    above = one_row(above, s_high, s_low)
    shared[...] = jnp.broadcast_to(jnp.where(lower, own, above), shared.shape)
    middle = jnp.concatenate([middle, jnp.zeros((12, 128), F32)], axis=0).astype(BF16)
    block[16:32, 0:128] = middle
    block[16:32, 128:256] = middle


def far_kernel(
    table, own, below, above, shared, picks_hbm, m2l, root_ops, boxes, roots,
    picks, near, base, shifted, sem,
):
    me = lax.axis_index(AXIS)
    place = me % 4
    fetch = pltpu.make_async_copy(picks_hbm.at[place], picks, sem)
    fetch.start()

    lanes = lax.broadcasted_iota(jnp.int32, (1, 128), 1)
    lower = lanes < RANK
    gathered = shared[...]
    high_half = jnp.sum(gathered.reshape(NROOT, 8, 128), axis=1).astype(BF16).astype(F32)
    low_half = pltpu.roll(high_half, RANK, 1)
    base[...] = jnp.zeros(base.shape, F32)
    shifted[...] = jnp.zeros(shifted.shape, F32)
    base[32:64, :] = jnp.where(lower, low_half, 0.0)
    shifted[31:63, :] = jnp.where(lower, 0.0, high_half)
    base[...] = base[...] + shifted[...]
    total = jnp.zeros((NROOT, RANK), F32)
    for distance in range(-31, 32, 2):
        if distance == -1:
            continue
        source = base[32 + distance : 64 + distance, :]
        first = distance + NROOT - 1
        if distance == 1:
            source = jnp.where(lower, 0.0, source)
        if distance == 31:
            total = total + dot(source[:, :RANK].astype(BF16), root_ops[first])
            continue
        operator = jnp.concatenate([root_ops[first], root_ops[first + 1]], axis=0)
        total = total + dot(source.astype(BF16), operator)
    roots[...] = total

    row_of = me % 8
    first_column = me // 8 * 2
    columns_total = lax.axis_size(AXIS) // 4
    far = jnp.zeros((8, RANK), F32)
    for n in range(3):
        column = first_column + table[row_of, 12 + n]
        inside = jnp.logical_and(column >= 0, column < columns_total)
        kept = jnp.where(inside, 1.0, 0.0).astype(F32)
        start = jnp.clip(column, 0, columns_total - 1) * 4
        for other in range(4):
            source = shared[pl.ds(start + other, 1), :][:, :RANK] * kept
            source = jnp.broadcast_to(source, (8, RANK)).astype(BF16)
            far = far + dot(source, m2l[table[row_of, n * 4 + other]])
    boxes[0:1, :] = far[0:1]

    x01, x23, x45, x67 = below[...], own[:, 0:128], own[:, 128:256], above[...]

    def crossed(a, b):
        return jnp.where(lower, pltpu.roll(a, RANK, 1), pltpu.roll(b, RANK, 1))

    x01, x23, x45, x67 = (x.astype(F32) for x in (x01, x23, x45, x67))
    none = jnp.zeros_like(x01)
    blocks = [
        x01, x23, x45, x67,
        crossed(x01, x23), crossed(x23, x45), crossed(x45, x67),
        crossed(none, x01), crossed(none, x23), crossed(x45, none), crossed(x67, none),
    ]
    wide = jnp.concatenate(blocks, axis=1).astype(BF16)
    fetch.wait()
    near[...] = dot(picks[...], wide).astype(BF16)

    def part(pair, rows, which):
        if which is None:
            return jnp.zeros((16, 128), BF16)
        first = pair * 32 + rows
        return near[first : first + 16, which * 128 : which * 128 + 128]

    even = {0: (7, 4, 5, 9), 1: (8, 5, 6, 10)}
    odd = {0: (0, 1, 2, None), 1: (1, 2, 3, None)}
    even_far = {0: (7, 2), 1: (8, 3)}
    odd_far = {0: (0, 9), 1: (1, 10)}
    level1 = ((7, 4, 6, 10), (0, 1, 3, None))
    level1_far = ((7, 3), (0, 10))
    first_rows = lax.broadcasted_iota(jnp.int32, (16, 128), 0) < 4
    total = jnp.zeros((80, RANK), F32)
    for pair in range(49):
        v, w = pair // 7 - 3, pair % 7 - 3
        close = max(abs(v), abs(w)) < 2
        shifts = (-3, -2, 2, 3) if close else range(-3, 4)
        e, o, l1 = (even_far, odd_far, level1_far) if close else (even, odd, level1)
        rows = []
        for halves in (e, o):
            for a in range(2):
                rows.append(jnp.concatenate([part(pair, 0, k) for k in halves[a]], axis=1))
        both = [
            jnp.where(first_rows, part(pair, 16, a).astype(F32), part(pair, 16, b).astype(F32)).astype(BF16)
            for a, b in zip(*l1)
        ]
        rows.append(jnp.concatenate(both, axis=1))
        left = jnp.concatenate(rows, axis=0)
        operator = [m2l[DIRS[(u, v, w)]] for u in shifts]
        if not close:
            left = left[:, : 7 * RANK]
        total = total + dot(left, jnp.concatenate(operator, axis=0))
    boxes[1:9, :] = total[64:72]
    for p in range(2):
        for a in range(2):
            x = 2 * a + p
            first = (p * 2 + a) * 16
            boxes[9 + 16 * x : 25 + 16 * x, :] = total[first : first + 16]


def whole(space=pltpu.VMEM):
    return pl.BlockSpec(memory_space=space)


def upward(offsets, forces, counts, uc2ue, m2m_ops, compress):
    devices = lax.axis_size(AXIS)
    points = surface_points().astype(np.float32)
    spread = np.zeros((4, NQ, P_CAP), np.float32)
    spread[:3] = points[:, :, None]
    rows = np.zeros((8, NQ), np.float32)
    rows[:3] = points

    def kernel(off, frc, cnt, surf, pts, order, uc, m2m_hbm, comp, shared, block, *scratch):
        surface = [surf.at[0], surf.at[1], surf.at[2], pts]
        wrapped = Surface(surface)
        upward_kernel(off, frc, cnt, wrapped, order, uc, m2m_hbm, comp, shared, block, *scratch)

    return pl.pallas_call(
        kernel,
        out_shape=(
            jax.ShapeDtypeStruct((devices, 128), F32),
            jax.ShapeDtypeStruct((32, 256), BF16),
        ),
        in_specs=[
            whole(), whole(), whole(pltpu.SMEM), whole(), whole(), whole(), whole(),
            whole(pl.ANY), whole(),
        ],
        out_specs=(whole(), whole()),
        scratch_shapes=[
            pltpu.VMEM((8, NCOEF, NCOEF), F32),
            pltpu.VMEM((8, NCOEF, NCOEF), BF16),
            pltpu.VMEM((8, NCOEF, NCOEF), BF16),
            pltpu.VMEM((LEAF_DEV, 4, NQ), F32),
            pltpu.SemaphoreType.DMA,
        ],
        compiler_params=pltpu.CompilerParams(vmem_limit_bytes=40 * 2**20),
        name="upward",
    )(
        offsets, forces, counts, jnp.asarray(spread[:3]), jnp.asarray(rows),
        jnp.asarray(leaf_order()), uc2ue, m2m_ops, compress,
    )


class Surface:
    def __init__(self, refs):
        self.refs = refs

    def __getitem__(self, s):
        return self.refs[s][...] if s < 3 else self.refs[3]


def far_field(own, below, above, shared, m2l_ops, root_ops):
    return pl.pallas_call(
        far_kernel,
        out_shape=(
            jax.ShapeDtypeStruct((BOX_DEV, RANK), F32),
            jax.ShapeDtypeStruct((NROOT, RANK), F32),
        ),
        in_specs=[
            whole(pltpu.SMEM), whole(), whole(), whole(), whole(), whole(pl.ANY), whole(), whole(),
        ],
        out_specs=(whole(), whole()),
        scratch_shapes=[
            pltpu.VMEM((49 * 32, 128), BF16),
            pltpu.VMEM((49 * 32, 11 * 128), BF16),
            pltpu.VMEM((96, 128), F32),
            pltpu.VMEM((96, 128), F32),
            pltpu.SemaphoreType.DMA,
        ],
        compiler_params=pltpu.CompilerParams(vmem_limit_bytes=40 * 2**20),
        name="far_field",
    )(
        jnp.asarray(device_level_table()), own, below, above, shared,
        jnp.asarray(cross_section_picks()), m2l_ops, root_ops,
    )


def swapped(value, mask):
    devices = lax.axis_size(AXIS)
    return lax.ppermute(value, AXIS, [(s, s ^ mask) for s in range(devices)])


def swapped_between(value, unit):
    devices = lax.axis_size(AXIS)
    pairs = []
    for s in range(devices):
        b, r = divmod(s, unit)
        t = b + 1 if b % 2 == 1 else b - 1
        if 0 <= t < devices // unit:
            pairs.append((s, t * unit + r))
    return lax.ppermute(value, AXIS, pairs)


def body(offsets, forces, counts, uc2ue, m2m_ops, compress, m2l_ops, root_ops):
    me = lax.axis_index(AXIS)
    shared, block = upward(offsets, forces, counts, uc2ue, m2m_ops, compress)
    shared = lax.all_to_all(shared, AXIS, 0, 0, tiled=True)
    two = jnp.concatenate([block, swapped(block, 1)], axis=0)
    own = jnp.concatenate([two, swapped(two, 2)], axis=0)
    pair = swapped(own, 6)
    pair = jnp.concatenate([pair[64:], pair[:64]], axis=0)
    is_upper = me // 4 % 2 == 1
    root_even = me // 8 % 2 == 0
    upper_rim = jnp.where(is_upper, own[:, 128:], pair[:, 128:])
    lower_rim = jnp.where(is_upper, pair[:, :128], own[:, :128])
    inner = swapped(jnp.where(root_even, upper_rim, lower_rim), 8)
    outer = swapped_between(jnp.where(root_even, lower_rim, upper_rim), 8)
    from_below = jnp.where(root_even, outer, inner)
    from_above = jnp.where(root_even, inner, outer)
    below = jnp.where(is_upper, pair[:, 128:], from_below)
    above = jnp.where(is_upper, from_above, pair[:, :128])
    return far_field(own, below, above, shared, m2l_ops, root_ops)


def solution(mesh):
    placed = (P(None, AXIS), P(None, AXIS), P(AXIS), P(), P(), P(), P(), P())
    return jax.shard_map(
        body, mesh=mesh, in_specs=placed, out_specs=(P(AXIS, None), P()), check_vma=False
    )
```

profile of v0, /device:TPU:24, one launch (start us, length us, event | category | flops | bytes accessed | tf_op | source)
XLA Modules:
  0.0 68.7 jit_solution(1770727513922631298)
XLA Ops:
  0.6 1.0 %copy.18.comp = f32[456,64]{1,0:T(8,128)S(1)} copy(f32[456,64]{0,1:T(8,128)} %param.18) | data formatting | bytes 233472 | tf_op args[5]
  1.7 0.0 copy-start.1
  1.7 3.1 %copy-done.1 = f32[8,456,456]{2,1,0:T(8,128)S(1)} copy-done((f32[8,456,456]{2,1,0:T(8,128)S(1)}, f32[8,456,456]{2,1,0:T(8,128)}, u32[]{:S(2)}) %copy-start.1) | copy-done | bytes 6653976
  4.8 0.0 copy-start.4
  4.8 1.2 %copy-done.4 = f32[456,456]{1,0:T(8,128)S(1)} copy-done((f32[456,456]{1,0:T(8,128)S(1)}, f32[456,456]{1,0:T(8,128)}, u32[]{:S(2)}) %copy-start.4) | copy-done | bytes 831768
  6.0 0.0 copy-start.5
  6.0 0.9 %copy-done.5 = f32[3,152,128]{2,1,0:T(8,128)S(1)} copy-done((f32[3,152,128]{2,1,0:T(8,128)S(1)}, f32[3,152,128]{2,1,0:T(8,128)}, u32[]{:S(2)}) %copy-start.5) | copy-done | bytes 233496
  6.9 0.0 copy-start.6
  6.9 0.9 %copy-done.6 = f32[3,8192]{1,0:T(4,128)S(1)} copy-done((f32[3,8192]{1,0:T(4,128)S(1)}, f32[3,8192]{1,0:T(4,128)}, u32[]{:S(2)}) %copy-start.6) | copy-done | bytes 98328
  7.8 0.0 copy-start.7
  7.8 0.9 %copy-done.7 = f32[3,8192]{1,0:T(4,128)S(1)} copy-done((f32[3,8192]{1,0:T(4,128)S(1)}, f32[3,8192]{1,0:T(4,128)}, u32[]{:S(2)}) %copy-start.7) | copy-done | bytes 98328
  8.7 0.0 copy-start.8
  8.7 0.7 %copy-done.8 = bf16[64,64]{1,0:T(8,128)(2,1)S(1)} copy-done((bf16[64,64]{1,0:T(8,128)(2,1)S(1)}, bf16[64,64]{1,0:T(8,128)(2,1)}, u32[]{:S(2)}) %copy-start.8) | copy-done | bytes 8216
  9.4 0.0 copy-start.9
  9.4 0.7 %copy-done.9 = f32[8,152]{1,0:T(8,128)S(1)} copy-done((f32[8,152]{1,0:T(8,128)S(1)}, f32[8,152]{1,0:T(8,128)}, u32[]{:S(2)}) %copy-start.9) | copy-done | bytes 4888
  10.1 0.0 copy-start.11
  10.1 0.7 copy-done.11
  10.8 11.7 %upward.1 = (f32[256,128]{1,0:T(8,128)}, bf16[32,256]{1,0:T(8,128)(2,1)S(1)}) custom-call(f32[3,8192]{1,0:T(4,128)S(1)} %copy-done.6, f32[3,8192]{1,0:T(4,128)S(1)} %copy-done.7, s32[64]{0:T(128)S(1)} %copy-done.11, f32[3,152,128]{2,1,0:T(8,128)S(1)} %copy-done.5, f32[8,152]{1,0:T(8,128)S(1)} %copy-done.9, bf16[64,64]{1,0:T(8,128)(2,1)S(1)} %copy-done.8, ...), custom_call_target="tpu_custom_call" | custom-call | tf_op jit(solution)/shard_map/upward/pallas_call | solution.py:330
  22.5 0.0 copy-start.2
  22.5 0.0 copy-start.3
  22.5 0.0 copy-start.10
  22.5 0.1 collective-permute-start
  22.6 1.2 %collective-permute-done = bf16[32,256]{1,0:T(8,128)(2,1)S(1)} collective-permute-done((bf16[32,256]{1,0:T(8,128)(2,1)S(1)}, bf16[32,256]{1,0:T(8,128)(2,1)S(1)}, u32[]{:S(2)}, u32[]{:S(2)}) %collective-permute-start) | collective-permute-done | bytes 16416 | tf_op jit(solution)/shard_map/ppermute | solution.py:392
  23.8 1.5 %collective-permute-start.1 = (bf16[64,256]{1,0:T(8,128)(2,1)S(1)}, bf16[64,256]{1,0:T(8,128)(2,1)S(1)}, u32[]{:S(2)}, u32[]{:S(2)}) collective-permute-start(bf16[64,256]{1,0:T(8,128)(2,1)S(1)} %pad_maximum_fusion.1), channel_id=1, source_target_pairs={{0,2},{1,3},{2,0},{3,1},{4,6},{5,7},{6,4},{7,5},{8,10},{9,11},{10,... | collective-permute-start | bytes 98312 | tf_op jit(solution)/shard_map/ppermute | solution.py:392
  25.3 2.4 %collective-permute-done.1 = bf16[64,256]{1,0:T(8,128)(2,1)S(1)} collective-permute-done((bf16[64,256]{1,0:T(8,128)(2,1)S(1)}, bf16[64,256]{1,0:T(8,128)(2,1)S(1)}, u32[]{:S(2)}, u32[]{:S(2)}) %collective-permute-start.1) | collective-permute-done | bytes 32800 | tf_op jit(solution)/shard_map/ppermute | solution.py:392
  27.7 2.8 %collective-permute-start.2 = (bf16[128,256]{1,0:T(8,128)(2,1)S(1)}, bf16[128,256]{1,0:T(8,128)(2,1)S(1)}, u32[]{:S(2)}, u32[]{:S(2)}) collective-permute-start(bf16[128,256]{1,0:T(8,128)(2,1)S(1)} %constant_dynamic-update-slice_fusion.own), channel_id=1, source_target_pairs={{0,6},{1,7},{2,4},{3,5},{4,2},{5,3},{6,0},{7,1},{8,14},{9,15},{10,... | collective-permute-start | bytes 196616 | tf_op jit(solution)/shard_map/ppermute | solution.py:392
  30.5 12.2 %all-to-all-start = ((f32[256,1,128]{2,1,0:T(1,128)}), f32[256,1,128]{2,1,0:T(1,128)S(1)}, u32[]{:S(2)}, u32[]{:S(2)}) async-start(f32[256,1,128]{2,1,0:T(1,128)} %bitcast.1), calls=%async_computation | async-start | bytes 262144 | tf_op jit(solution)/shard_map/all_to_all | solution.py:409
  42.7 0.0 collective-permute-done.2
  42.8 1.8 %collective-permute-start.4 = (bf16[128,128]{1,0:T(8,128)(2,1)S(1)}, bf16[128,128]{1,0:T(8,128)(2,1)S(1)}, u32[]{:S(2)}, u32[]{:S(2)}) collective-permute-start(bf16[128,128]{1,0:T(8,128)(2,1)S(1)} %get-tuple-element.12), channel_id=1, source_target_pairs={{0,8},{1,9},{2,10},{3,11},{4,12},{5,13},{6,14},{7,15},{8,0},{9,1},... | collective-permute-start | bytes 98312 | tf_op jit(solution)/shard_map/ppermute | solution.py:392
  44.6 6.1 %collective-permute-start.3 = (bf16[128,128]{1,0:T(8,128)(2,1)S(1)}, bf16[128,128]{1,0:T(8,128)(2,1)S(1)}, u32[]{:S(2)}, u32[]{:S(2)}) collective-permute-start(bf16[128,128]{1,0:T(8,128)(2,1)S(1)} %get-tuple-element.13), channel_id=1, source_target_pairs={{8,16},{9,17},{10,18},{11,19},{12,20},{13,21},{14,22},{15,23},{16,... | collective-permute-start | bytes 98312 | tf_op jit(solution)/shard_map/ppermute | solution.py:403
  50.8 10.1 %copy.20.m2l = bf16[316,64,64]{2,1,0:T(8,128)(2,1)} copy(bf16[316,64,64]{0,2,1:T(8,128)(2,1)} %param.19) | data formatting | bytes 5177344 | tf_op args[6]
  60.8 0.0 collective-permute-done.4
  60.8 0.0 collective-permute-done.3
  60.8 0.0 all-to-all-done
  60.9 0.0 copy-done.2
  60.9 0.0 copy-done.3
  60.9 0.0 copy-done.10
  60.9 0.0 copy-start
  60.9 2.5 %copy-done = bf16[316,64,64]{2,1,0:T(8,128)(2,1)S(1)} copy-done((bf16[316,64,64]{2,1,0:T(8,128)(2,1)S(1)}, bf16[316,64,64]{2,1,0:T(8,128)(2,1)}, u32[]{:S(2)}) %copy-start) | copy-done | bytes 2588696
  63.4 4.6 %far_field.1 = (f32[73,64]{1,0:T(8,128)S(1)}, f32[32,64]{1,0:T(8,128)}) custom-call(s32[8,24]{1,0:T(8,128)S(1)} %copy-done.10, bf16[128,256]{1,0:T(8,128)(2,1)S(1)} %constant_dynamic-update-slice_fusion.own, bf16[128,128]{1,0:T(8,128)(2,1)S(1)} %get-tuple-element.11.below, bf16[128,128]{1,0:T(8,128)(2,1)S(1)} %get-tuple-element.10.above, ...), custom_call_target="tpu_custom_call" | custom-call | tf_op jit(solution)/shard_map/far_field/pallas_call | solution.py:365
  68.0 0.7 %copy.21 = f32[73,64]{0,1:T(8,128)} copy(f32[73,64]{1,0:T(8,128)S(1)} %get-tuple-element.8) | data formatting | bytes 37376 | tf_op jit(solution)/shard_map/far_field/pallas_call | solution.py:365
  (7 shorter events, 0.1 us)
Async XLA Ops:
  1.7 3.1 %copy-start.1 = (f32[8,456,456]{2,1,0:T(8,128)S(1)}, f32[8,456,456]{2,1,0:T(8,128)}, u32[]{:S(2)}) copy-start(f32[8,456,456]{2,1,0:T(8,128)} %m2m_hbm.1) | copy-start | bytes 19961860
  4.8 1.2 %copy-start.4 = (f32[456,456]{1,0:T(8,128)S(1)}, f32[456,456]{1,0:T(8,128)}, u32[]{:S(2)}) copy-start(f32[456,456]{1,0:T(8,128)} %uc.1) | copy-start | bytes 2495236
  6.0 0.9 %copy-start.5 = (f32[3,152,128]{2,1,0:T(8,128)S(1)}, f32[3,152,128]{2,1,0:T(8,128)}, u32[]{:S(2)}) copy-start(f32[3,152,128]{2,1,0:T(8,128)} %constant.56.clone.surf) | copy-start | bytes 700420
  6.9 0.9 %copy-start.6 = (f32[3,8192]{1,0:T(4,128)S(1)}, f32[3,8192]{1,0:T(4,128)}, u32[]{:S(2)}) copy-start(f32[3,8192]{1,0:T(4,128)} %off.1) | copy-start | bytes 294916
  7.8 0.9 %copy-start.7 = (f32[3,8192]{1,0:T(4,128)S(1)}, f32[3,8192]{1,0:T(4,128)}, u32[]{:S(2)}) copy-start(f32[3,8192]{1,0:T(4,128)} %frc.1) | copy-start | bytes 294916
  8.7 0.7 %copy-start.8 = (bf16[64,64]{1,0:T(8,128)(2,1)S(1)}, bf16[64,64]{1,0:T(8,128)(2,1)}, u32[]{:S(2)}) copy-start(bf16[64,64]{1,0:T(8,128)(2,1)} %constant.58.clone.order) | copy-start | bytes 24580
  9.4 0.7 %copy-start.9 = (f32[8,152]{1,0:T(8,128)S(1)}, f32[8,152]{1,0:T(8,128)}, u32[]{:S(2)}) copy-start(f32[8,152]{1,0:T(8,128)} %constant.57.clone.pts) | copy-start | bytes 14596
  10.1 0.7 copy-start.11
  22.5 38.4 %copy-start.2 = (bf16[4,1568,128]{2,1,0:T(8,128)(2,1)S(1)}, bf16[4,1568,128]{2,1,0:T(8,128)(2,1)}, u32[]{:S(2)}) copy-start(bf16[4,1568,128]{2,1,0:T(8,128)(2,1)} %constant.60.clone.picks_hbm) | copy-start | bytes 4816900
  22.5 38.4 %copy-start.3 = (bf16[63,64,64]{2,1,0:T(8,128)(2,1)S(1)}, bf16[63,64,64]{2,1,0:T(8,128)(2,1)}, u32[]{:S(2)}) copy-start(bf16[63,64,64]{2,1,0:T(8,128)(2,1)} %root_ops.1) | copy-start | bytes 1548292
  22.5 38.4 %copy-start.10 = (s32[8,24]{1,0:T(8,128)S(1)}, s32[8,24]{1,0:T(8,128)}, u32[]{:S(2)}) copy-start(s32[8,24]{1,0:T(8,128)} %constant.59.clone.table) | copy-start | bytes 2308
  22.5 1.3 %collective-permute-start = (bf16[32,256]{1,0:T(8,128)(2,1)S(1)}, bf16[32,256]{1,0:T(8,128)(2,1)S(1)}, u32[]{:S(2)}, u32[]{:S(2)}) collective-permute-start(bf16[32,256]{1,0:T(8,128)(2,1)S(1)} %get-tuple-element.4), channel_id=1, source_target_pairs={{0,1},{1,0},{2,3},{3,2},{4,5},{5,4},{6,7},{7,6},{8,9},{9,8},{10,11... | collective-permute-start | bytes 49160 | tf_op jit(solution)/shard_map/ppermute | solution.py:392
  23.8 3.9 %collective-permute-start.1 = (bf16[64,256]{1,0:T(8,128)(2,1)S(1)}, bf16[64,256]{1,0:T(8,128)(2,1)S(1)}, u32[]{:S(2)}, u32[]{:S(2)}) collective-permute-start(bf16[64,256]{1,0:T(8,128)(2,1)S(1)} %pad_maximum_fusion.1), channel_id=1, source_target_pairs={{0,2},{1,3},{2,0},{3,1},{4,6},{5,7},{6,4},{7,5},{8,10},{9,11},{10,... | collective-permute-start | bytes 98312 | tf_op jit(solution)/shard_map/ppermute | solution.py:392
  27.7 15.0 %collective-permute-start.2 = (bf16[128,256]{1,0:T(8,128)(2,1)S(1)}, bf16[128,256]{1,0:T(8,128)(2,1)S(1)}, u32[]{:S(2)}, u32[]{:S(2)}) collective-permute-start(bf16[128,256]{1,0:T(8,128)(2,1)S(1)} %constant_dynamic-update-slice_fusion.own), channel_id=1, source_target_pairs={{0,6},{1,7},{2,4},{3,5},{4,2},{5,3},{6,0},{7,1},{8,14},{9,15},{10,... | collective-permute-start | bytes 196616 | tf_op jit(solution)/shard_map/ppermute | solution.py:392
  30.5 30.4 %all-to-all-start = ((f32[256,1,128]{2,1,0:T(1,128)}), f32[256,1,128]{2,1,0:T(1,128)S(1)}, u32[]{:S(2)}, u32[]{:S(2)}) async-start(f32[256,1,128]{2,1,0:T(1,128)} %bitcast.1), calls=%async_computation | async-start | bytes 262144 | tf_op jit(solution)/shard_map/all_to_all | solution.py:409
  42.8 18.0 %collective-permute-start.4 = (bf16[128,128]{1,0:T(8,128)(2,1)S(1)}, bf16[128,128]{1,0:T(8,128)(2,1)S(1)}, u32[]{:S(2)}, u32[]{:S(2)}) collective-permute-start(bf16[128,128]{1,0:T(8,128)(2,1)S(1)} %get-tuple-element.12), channel_id=1, source_target_pairs={{0,8},{1,9},{2,10},{3,11},{4,12},{5,13},{6,14},{7,15},{8,0},{9,1},... | collective-permute-start | bytes 98312 | tf_op jit(solution)/shard_map/ppermute | solution.py:392
  44.6 16.2 %collective-permute-start.3 = (bf16[128,128]{1,0:T(8,128)(2,1)S(1)}, bf16[128,128]{1,0:T(8,128)(2,1)S(1)}, u32[]{:S(2)}, u32[]{:S(2)}) collective-permute-start(bf16[128,128]{1,0:T(8,128)(2,1)S(1)} %get-tuple-element.13), channel_id=1, source_target_pairs={{8,16},{9,17},{10,18},{11,19},{12,20},{13,21},{14,22},{15,23},{16,... | collective-permute-start | bytes 98312 | tf_op jit(solution)/shard_map/ppermute | solution.py:403
  60.9 2.5 %copy-start = (bf16[316,64,64]{2,1,0:T(8,128)(2,1)S(1)}, bf16[316,64,64]{2,1,0:T(8,128)(2,1)}, u32[]{:S(2)}) copy-start(bf16[316,64,64]{2,1,0:T(8,128)(2,1)} %copy.20.m2l) | copy-start | bytes 7766020
where the time goes:
time: 69.3 us; the launch traced here: 68.7 us
  starting transfers between devices  24.5 us (35%)
  local copies, waits for them, and re-layouts  23.4 us (34%)
  Pallas kernels  16.2 us (23%)
  waiting for transfers between devices  3.59 us (5%)
  between operations  0.85 us (1%)
    unnamed x28, local copies, waits for them, and re-layouts  22.7 us
    all_to_all x1, starting transfers between devices, body(): shared = lax.all_to_all(shared, AXIS, 0, 0, tiled=True)  12.2 us
    pallas_call x1, Pallas kernels, upward(): pl.pallas_call(kernel, out_shape=(jax.ShapeDtypeStruct((devices, 128), F3...  11.7 us
    ppermute x4, starting transfers between devices, swapped(): return lax.ppermute(value, AXIS, [(s, s ^ mask) for s in range(devices)])  6.16 us
    ppermute x1, starting transfers between devices, swapped_between(): return lax.ppermute(value, AXIS, pairs)  6.14 us
    pallas_call x1, Pallas kernels, far_field(): pl.pallas_call(far_kernel, out_shape=(jax.ShapeDtypeStruct((BOX_DEV, RANK...  4.59 us
    ppermute x4, waiting for transfers between devices, swapped(): return lax.ppermute(value, AXIS, [(s, s ^ mask) for s in range(devices)])  3.59 us
  transfers between devices with their start and end apart: 6, of which 2 were waited for; matrix products, arithmetic and copies ran while one was open for 15% of the time, Pallas kernels for 0%

commit v1 on v0

--- a/solution.py
+++ b/solution.py
@@ -112,7 +112,11 @@
     return jnp.dot(a, b, preferred_element_type=F32)
 
 
-def product(x, w_high, w_low):
+def dot_nt(a, b):
+    return lax.dot_general(a, b, (((1,), (1,)), ((), ())), preferred_element_type=F32)
+
+
+def product(x, w_high, w_low, dot=dot):
     rows = x.shape[0]
     both = stacked(x)
     top = dot(both, w_high)
@@ -121,11 +125,21 @@
 
 
 def upward_kernel(
-    offsets, forces, counts, surface, order, uc2ue, m2m_hbm, compress, shared, block,
-    m2m, m2m_high, m2m_low, check, sem,
+    offsets_hbm, forces_hbm, counts_hbm, surface_hbm, points_hbm, order_hbm, uc2ue_hbm, m2m_hbm,
+    compress_hbm, shared, block,
+    offsets, forces, counts, surface, points, order, uc2ue, m2m, compress,
+    m2m_high, m2m_low, check, sems,
 ):
-    fetch = pltpu.make_async_copy(m2m_hbm, m2m, sem)
-    fetch.start()
+    pairs = (
+        (offsets_hbm, offsets), (forces_hbm, forces), (counts_hbm, counts), (surface_hbm, surface),
+        (points_hbm, points), (order_hbm, order), (uc2ue_hbm, uc2ue), (compress_hbm, compress),
+        (m2m_hbm, m2m),
+    )
+    fetches = [pltpu.make_async_copy(a, b, sems.at[n]) for n, (a, b) in enumerate(pairs)]
+    for fetch in fetches:
+        fetch.start()
+    for fetch in fetches[:4]:
+        fetch.wait()
     slots = lax.broadcasted_iota(jnp.int32, (1, P_CAP), 1)
     zero = jnp.zeros((1, P_CAP), F32)
     one = jnp.ones((1, P_CAP), F32)
@@ -145,9 +159,8 @@
             [jnp.concatenate([f, zero], axis=0), jnp.concatenate([-u, one], axis=0)], axis=1
         )
         left = stacked(left)
-        nt = (((1,), (1,)), ((), ()))
-        top = lax.dot_general(left, high.astype(BF16), nt, preferred_element_type=F32)
-        rest = lax.dot_general(left, low.astype(BF16), nt, preferred_element_type=F32)
+        top = dot_nt(left, high.astype(BF16))
+        rest = dot_nt(left, low.astype(BF16))
         sums = top[0:4] + (top[4:8] + rest[0:4])
         octant = (l >> 4 & 1) * 4 + (l >> 2 & 1) * 2 + (l & 1)
         parent = (l >> 5 & 1) * 4 + (l >> 3 & 1) * 2 + (l >> 1 & 1)
@@ -156,23 +169,24 @@
 
     lax.fori_loop(0, LEAF_DEV, leaf, 0, unroll=LEAF_UNROLL)
 
-    points = surface[3][:, :]
+    for fetch in fetches[4:8]:
+        fetch.wait()
     density = jnp.zeros((LEAF_DEV, NCOEF), F32)
     for s in range(3):
         rows = check[:, s, :] + check[:, 3, :] * points[s : s + 1, :]
         w_high, w_low = split(uc2ue[s * NQ : (s + 1) * NQ, :])
         density = density + product(rows, w_high.astype(BF16), w_low.astype(BF16))
     shrink = compress[...]
-    shrink = jnp.concatenate([shrink, shrink], axis=1)
+    shrink = jnp.concatenate([shrink, shrink], axis=0)
     s_high, s_low = split(shrink)
     s_high, s_low = s_high.astype(BF16), s_low.astype(BF16)
     lower = lax.broadcasted_iota(jnp.int32, (1, 128), 1) < RANK
-    leaves = product(density, s_high, s_low).astype(BF16)
+    leaves = product(density, s_high, s_low, dot_nt).astype(BF16)
     leaves = dot(order[...], leaves)
     block[0:16, 0:128] = jnp.where(lower, leaves[0:16], leaves[16:32]).astype(BF16)
     block[0:16, 128:256] = jnp.where(lower, leaves[32:48], leaves[48:64]).astype(BF16)
 
-    fetch.wait()
+    fetches[8].wait()
     parents = jnp.zeros((8, NCOEF), F32)
     for o in range(8):
         w_high, w_low = split(m2m[o])
@@ -180,10 +194,10 @@
         m2m_high[o] = w_high
         m2m_low[o] = w_low
         parents = parents + product(density[o * 8 : o * 8 + 8], w_high, w_low)
-    middle = product(parents, s_high, s_low).astype(BF16).astype(F32)
+    middle = product(parents, s_high, s_low, dot_nt).astype(BF16).astype(F32)
     middle = jnp.where(lower, middle[0:4], middle[4:8])
 
-    def one_row(x, w_high, w_low):
+    def one_row(x, w_high, w_low, dot=dot):
         high, low = split(x)
         row = lax.broadcasted_iota(jnp.int32, (8, 1), 0)
         both = jnp.where(row == 0, high, jnp.where(row == 1, low, 0.0)).astype(BF16)
@@ -194,64 +208,46 @@
     device = jnp.zeros((1, NCOEF), F32)
     for o in range(8):
         device = device + one_row(parents[o : o + 1], m2m_high[o], m2m_low[o])
-    own = one_row(device, s_high, s_low).astype(BF16).astype(F32)
+    own = one_row(device, s_high, s_low, dot_nt).astype(BF16).astype(F32)
     octant = lax.axis_index(AXIS) % 8
     above = one_row(device, m2m_high[octant], m2m_low[octant])
-    above = one_row(above, s_high, s_low)
+    above = one_row(above, s_high, s_low, dot_nt)
     shared[...] = jnp.broadcast_to(jnp.where(lower, own, above), shared.shape)
     middle = jnp.concatenate([middle, jnp.zeros((12, 128), F32)], axis=0).astype(BF16)
     block[16:32, 0:128] = middle
     block[16:32, 128:256] = middle
 
 
-def far_kernel(
-    table, own, below, above, shared, picks_hbm, m2l, root_ops, boxes, roots,
-    picks, near, base, shifted, sem,
-):
+def operators_kernel(source_hbm, out, source, turned, sem):
+    fetch = pltpu.make_async_copy(source_hbm, source, sem)
+    fetch.start()
+    directions = source.shape[2]
+    rows = (directions + 7) // 8 * 8
+    pitch = turned.shape[1] // 16
+    shape = (rows, directions)
+    unit = lax.broadcasted_iota(jnp.int32, shape, 0) == lax.broadcasted_iota(jnp.int32, shape, 1)
+    unit = unit.astype(F32).astype(BF16)
+    fetch.wait()
+    for g in range(16):
+        four = jnp.concatenate([source[g + 16 * part] for part in range(4)], axis=0)
+        moved = dot_nt(unit, four)
+        for half in range(2):
+            turned[half, g * pitch : g * pitch + rows, :] = moved[:, half * 128 : half * 128 + 128]
+    for d in range(directions):
+        parts = []
+        for half in range(2):
+            pair = turned[half, pl.ds(d, 16, stride=pitch), :]
+            parts += [pair, pltpu.roll(pair, RANK, 1)]
+        out[d] = jnp.concatenate(parts, axis=0)[:, :RANK].astype(BF16)
+
+
+def far_kernel(table, own, below, above, picks_hbm, m2l, boxes, device_ops, picks, near, sem):
     me = lax.axis_index(AXIS)
-    place = me % 4
-    fetch = pltpu.make_async_copy(picks_hbm.at[place], picks, sem)
+    fetch = pltpu.make_async_copy(picks_hbm.at[me % 4], picks, sem)
     fetch.start()
-
-    lanes = lax.broadcasted_iota(jnp.int32, (1, 128), 1)
-    lower = lanes < RANK
-    gathered = shared[...]
-    high_half = jnp.sum(gathered.reshape(NROOT, 8, 128), axis=1).astype(BF16).astype(F32)
-    low_half = pltpu.roll(high_half, RANK, 1)
-    base[...] = jnp.zeros(base.shape, F32)
-    shifted[...] = jnp.zeros(shifted.shape, F32)
-    base[32:64, :] = jnp.where(lower, low_half, 0.0)
-    shifted[31:63, :] = jnp.where(lower, 0.0, high_half)
-    base[...] = base[...] + shifted[...]
-    total = jnp.zeros((NROOT, RANK), F32)
-    for distance in range(-31, 32, 2):
-        if distance == -1:
-            continue
-        source = base[32 + distance : 64 + distance, :]
-        first = distance + NROOT - 1
-        if distance == 1:
-            source = jnp.where(lower, 0.0, source)
-        if distance == 31:
-            total = total + dot(source[:, :RANK].astype(BF16), root_ops[first])
-            continue
-        operator = jnp.concatenate([root_ops[first], root_ops[first + 1]], axis=0)
-        total = total + dot(source.astype(BF16), operator)
-    roots[...] = total
-
-    row_of = me % 8
-    first_column = me // 8 * 2
-    columns_total = lax.axis_size(AXIS) // 4
-    far = jnp.zeros((8, RANK), F32)
-    for n in range(3):
-        column = first_column + table[row_of, 12 + n]
-        inside = jnp.logical_and(column >= 0, column < columns_total)
-        kept = jnp.where(inside, 1.0, 0.0).astype(F32)
-        start = jnp.clip(column, 0, columns_total - 1) * 4
-        for other in range(4):
-            source = shared[pl.ds(start + other, 1), :][:, :RANK] * kept
-            source = jnp.broadcast_to(source, (8, RANK)).astype(BF16)
-            far = far + dot(source, m2l[table[row_of, n * 4 + other]])
-    boxes[0:1, :] = far[0:1]
+    lower = lax.broadcasted_iota(jnp.int32, (1, 128), 1) < RANK
+    for n in range(12):
+        device_ops[n] = m2l[table[me % 8, n]]
 
     x01, x23, x45, x67 = below[...], own[:, 0:128], own[:, 128:256], above[...]
 
@@ -302,6 +298,7 @@
         if not close:
             left = left[:, : 7 * RANK]
         total = total + dot(left, jnp.concatenate(operator, axis=0))
+    boxes[...] = jnp.zeros(boxes.shape, F32)
     boxes[1:9, :] = total[64:72]
     for p in range(2):
         for a in range(2):
@@ -310,6 +307,50 @@
             boxes[9 + 16 * x : 25 + 16 * x, :] = total[first : first + 16]
 
 
+def top_kernel(table, partial, device_ops, shared, root_ops, boxes, roots, base, shifted, turned):
+    me = lax.axis_index(AXIS)
+    lower = lax.broadcasted_iota(jnp.int32, (1, 128), 1) < RANK
+    gathered = shared[...]
+    high_half = jnp.sum(gathered.reshape(NROOT, 8, 128), axis=1).astype(BF16).astype(F32)
+    low_half = pltpu.roll(high_half, RANK, 1)
+    base[...] = jnp.zeros(base.shape, F32)
+    shifted[...] = jnp.zeros(shifted.shape, F32)
+    base[32:64, :] = jnp.where(lower, low_half, 0.0)
+    shifted[31:63, :] = jnp.where(lower, 0.0, high_half)
+    base[...] = base[...] + shifted[...]
+    total = jnp.zeros((NROOT, RANK), F32)
+    for distance in range(-31, 32, 2):
+        if distance == -1:
+            continue
+        source = base[32 + distance : 64 + distance, :]
+        first = distance + NROOT - 1
+        if distance == 1:
+            source = jnp.where(lower, 0.0, source)
+        if distance == 31:
+            total = total + dot(source[:, :RANK].astype(BF16), root_ops[first])
+            continue
+        operator = jnp.concatenate([root_ops[first], root_ops[first + 1]], axis=0)
+        total = total + dot(source.astype(BF16), operator)
+    roots[...] = total
+
+    first_column = me // 8 * 2
+    columns_total = lax.axis_size(AXIS) // 4
+    far = jnp.zeros((8, RANK), F32)
+    for n in range(3):
+        column = first_column + table[me % 8, 12 + n]
+        inside = jnp.logical_and(column >= 0, column < columns_total)
+        kept = jnp.where(inside, 1.0, 0.0).astype(F32)
+        start = jnp.clip(column, 0, columns_total - 1) * 4
+        for other in range(4):
+            source = shared[pl.ds(start + other, 1), :][:, :RANK] * kept
+            source = jnp.broadcast_to(source, (8, RANK)).astype(BF16)
+            far = far + dot(source, device_ops[n * 4 + other])
+    turned[...] = jnp.zeros(turned.shape, F32)
+    turned[0:80, 0:RANK] = partial[...]
+    turned[0:1, 0:RANK] = far[0:1]
+    boxes[...] = turned[...].T[:RANK, :BOX_DEV]
+
+
 def whole(space=pltpu.VMEM):
     return pl.BlockSpec(memory_space=space)
 
@@ -317,74 +358,89 @@
 def upward(offsets, forces, counts, uc2ue, m2m_ops, compress):
     devices = lax.axis_size(AXIS)
     points = surface_points().astype(np.float32)
-    spread = np.zeros((4, NQ, P_CAP), np.float32)
-    spread[:3] = points[:, :, None]
+    spread = np.ascontiguousarray(np.broadcast_to(points[:, :, None], (3, NQ, P_CAP)))
     rows = np.zeros((8, NQ), np.float32)
     rows[:3] = points
-
-    def kernel(off, frc, cnt, surf, pts, order, uc, m2m_hbm, comp, shared, block, *scratch):
-        surface = [surf.at[0], surf.at[1], surf.at[2], pts]
-        wrapped = Surface(surface)
-        upward_kernel(off, frc, cnt, wrapped, order, uc, m2m_hbm, comp, shared, block, *scratch)
-
+    operands = (
+        offsets, forces, counts, jnp.asarray(spread), jnp.asarray(rows), jnp.asarray(leaf_order()),
+        uc2ue, m2m_ops, compress.T,
+    )
+    held = [pltpu.VMEM(x.shape, x.dtype) for x in operands]
+    held[2] = pltpu.SMEM(counts.shape, counts.dtype)
     return pl.pallas_call(
-        kernel,
+        upward_kernel,
         out_shape=(
             jax.ShapeDtypeStruct((devices, 128), F32),
             jax.ShapeDtypeStruct((32, 256), BF16),
         ),
-        in_specs=[
-            whole(), whole(), whole(pltpu.SMEM), whole(), whole(), whole(), whole(),
-            whole(pl.ANY), whole(),
-        ],
+        in_specs=[whole(pltpu.HBM)] * len(operands),
         out_specs=(whole(), whole()),
-        scratch_shapes=[
-            pltpu.VMEM((8, NCOEF, NCOEF), F32),
+        scratch_shapes=held
+        + [
             pltpu.VMEM((8, NCOEF, NCOEF), BF16),
             pltpu.VMEM((8, NCOEF, NCOEF), BF16),
             pltpu.VMEM((LEAF_DEV, 4, NQ), F32),
-            pltpu.SemaphoreType.DMA,
+            pltpu.SemaphoreType.DMA((len(operands),)),
         ],
         compiler_params=pltpu.CompilerParams(vmem_limit_bytes=40 * 2**20),
         name="upward",
-    )(
-        offsets, forces, counts, jnp.asarray(spread[:3]), jnp.asarray(rows),
-        jnp.asarray(leaf_order()), uc2ue, m2m_ops, compress,
-    )
-
-
-class Surface:
-    def __init__(self, refs):
-        self.refs = refs
-
-    def __getitem__(self, s):
-        return self.refs[s][...] if s < 3 else self.refs[3]
-
-
-def far_field(own, below, above, shared, m2l_ops, root_ops):
+    )(*operands)
+
+
+def operators(m2l_ops):
+    count = m2l_ops.shape[0]
+    return pl.pallas_call(
+        operators_kernel,
+        out_shape=jax.ShapeDtypeStruct(m2l_ops.shape, BF16),
+        in_specs=[whole(pltpu.HBM)],
+        out_specs=whole(),
+        scratch_shapes=[
+            pltpu.VMEM((RANK, RANK, count), BF16),
+            pltpu.VMEM((2, 16 * (count + 5), 128), F32),
+            pltpu.SemaphoreType.DMA,
+        ],
+        compiler_params=pltpu.CompilerParams(vmem_limit_bytes=28 * 2**20),
+        name="operators",
+    )(jnp.transpose(m2l_ops, (1, 2, 0)))
+
+
+def far_field(table, own, below, above, m2l):
     return pl.pallas_call(
         far_kernel,
         out_shape=(
-            jax.ShapeDtypeStruct((BOX_DEV, RANK), F32),
-            jax.ShapeDtypeStruct((NROOT, RANK), F32),
+            jax.ShapeDtypeStruct((80, RANK), F32),
+            jax.ShapeDtypeStruct((12, RANK, RANK), BF16),
         ),
-        in_specs=[
-            whole(pltpu.SMEM), whole(), whole(), whole(), whole(), whole(pl.ANY), whole(), whole(),
-        ],
+        in_specs=[whole(pltpu.SMEM), whole(), whole(), whole(), whole(pltpu.HBM), whole()],
         out_specs=(whole(), whole()),
         scratch_shapes=[
             pltpu.VMEM((49 * 32, 128), BF16),
             pltpu.VMEM((49 * 32, 11 * 128), BF16),
+            pltpu.SemaphoreType.DMA,
+        ],
+        compiler_params=pltpu.CompilerParams(vmem_limit_bytes=28 * 2**20),
+        name="far_field",
+    )(table, own, below, above, jnp.asarray(cross_section_picks()), m2l)
+
+
+def top_levels(table, partial, device_ops, shared, root_ops):
+    boxes, roots = pl.pallas_call(
+        top_kernel,
+        out_shape=(
+            jax.ShapeDtypeStruct((RANK, BOX_DEV), F32),
+            jax.ShapeDtypeStruct((NROOT, RANK), F32),
+        ),
+        in_specs=[whole(pltpu.SMEM)] + [whole()] * 4,
+        out_specs=(whole(), whole()),
+        scratch_shapes=[
             pltpu.VMEM((96, 128), F32),
             pltpu.VMEM((96, 128), F32),
-            pltpu.SemaphoreType.DMA,
+            pltpu.VMEM((128, 128), F32),
         ],
-        compiler_params=pltpu.CompilerParams(vmem_limit_bytes=40 * 2**20),
-        name="far_field",
-    )(
-        jnp.asarray(device_level_table()), own, below, above, shared,
-        jnp.asarray(cross_section_picks()), m2l_ops, root_ops,
-    )
+        compiler_params=pltpu.CompilerParams(vmem_limit_bytes=16 * 2**20),
+        name="top_levels",
+    )(table, partial, device_ops, shared, root_ops)
+    return boxes.T, roots
 
 
 def swapped(value, mask):
@@ -421,7 +477,9 @@
     from_above = jnp.where(root_even, inner, outer)
     below = jnp.where(is_upper, pair[:, 128:], from_below)
     above = jnp.where(is_upper, from_above, pair[:, :128])
-    return far_field(own, below, above, shared, m2l_ops, root_ops)
+    table = jnp.asarray(device_level_table())
+    partial, device_ops = far_field(table, own, below, above, operators(m2l_ops))
+    return top_levels(table, partial, device_ops, shared, root_ops)
 
 
 def solution(mesh):

time: 69.3 us -> 59.9 us (0.86)
  the two profiles are of different devices: /device:TPU:24 before, /device:TPU:1 now
where the time goes in v1:
time: 59.9 us; the launch traced here: 59 us
  Pallas kernels  20.2 us (34%)
  starting transfers between devices  20.2 us (34%)
  local copies, waits for them, and re-layouts  10.1 us (17%)
  waiting for transfers between devices  7.63 us (13%)
  between operations  0.85 us (1%)
    all_to_all x1, starting transfers between devices, body(): shared = lax.all_to_all(shared, AXIS, 0, 0, tiled=True)  13.7 us
    pallas_call x1, Pallas kernels, upward(): pl.pallas_call(upward_kernel, out_shape=(jax.ShapeDtypeStruct((devices, 1...  12.2 us
    unnamed x28, local copies, waits for them, and re-layouts  10 us
    ppermute x4, starting transfers between devices, swapped(): return lax.ppermute(value, AXIS, [(s, s ^ mask) for s in range(devices)])  5.67 us
    all_to_all x1, waiting for transfers between devices, body(): shared = lax.all_to_all(shared, AXIS, 0, 0, tiled=True)  4.03 us
    ppermute x4, waiting for transfers between devices, swapped(): return lax.ppermute(value, AXIS, [(s, s ^ mask) for s in range(devices)])  3.6 us
    pallas_call x1, Pallas kernels, far_field(): pl.pallas_call(far_kernel, out_shape=(jax.ShapeDtypeStruct((80, RANK), F3...  3.37 us
    pallas_call x1, Pallas kernels, operators(): pl.pallas_call(operators_kernel, out_shape=jax.ShapeDtypeStruct(m2l_ops.s...  2.85 us
  transfers between devices with their start and end apart: 6, of which 3 were waited for; matrix products, arithmetic and copies ran while one was open for 0% of the time, Pallas kernels for 11%

profile of v1, /device:TPU:1, one launch (start us, length us, event | category | flops | bytes accessed | tf_op | source)
XLA Modules:
  0.0 59.0 jit_solution(14249117134568293220)
XLA Ops:
  0.6 0.0 copy-start
  0.6 3.1 %copy-done = f32[8,456,456]{2,1,0:T(8,128)S(1)} copy-done((f32[8,456,456]{2,1,0:T(8,128)S(1)}, f32[8,456,456]{2,1,0:T(8,128)}, u32[]{:S(2)}) %copy-start) | copy-done | bytes 6653976
  3.8 0.0 copy-start.4
  3.8 1.2 %copy-done.4 = f32[456,456]{1,0:T(8,128)S(1)} copy-done((f32[456,456]{1,0:T(8,128)S(1)}, f32[456,456]{1,0:T(8,128)}, u32[]{:S(2)}) %copy-start.4) | copy-done | bytes 831768
  4.9 0.0 copy-start.5
  4.9 0.9 %copy-done.5 = f32[3,152,128]{2,1,0:T(8,128)S(1)} copy-done((f32[3,152,128]{2,1,0:T(8,128)S(1)}, f32[3,152,128]{2,1,0:T(8,128)}, u32[]{:S(2)}) %copy-start.5) | copy-done | bytes 233496
  5.9 0.0 copy-start.6
  5.9 0.9 %copy-done.6 = f32[3,8192]{1,0:T(4,128)S(1)} copy-done((f32[3,8192]{1,0:T(4,128)S(1)}, f32[3,8192]{1,0:T(4,128)}, u32[]{:S(2)}) %copy-start.6) | copy-done | bytes 98328
  6.8 0.0 copy-start.7
  6.8 0.9 %copy-done.7 = f32[3,8192]{1,0:T(4,128)S(1)} copy-done((f32[3,8192]{1,0:T(4,128)S(1)}, f32[3,8192]{1,0:T(4,128)}, u32[]{:S(2)}) %copy-start.7) | copy-done | bytes 98328
  7.7 0.0 copy-start.8
  7.7 0.9 %copy-done.8 = f32[456,64]{0,1:T(8,128)S(1)} copy-done((f32[456,64]{0,1:T(8,128)S(1)}, f32[456,64]{0,1:T(8,128)}, u32[]{:S(2)}) %copy-start.8) | copy-done | bytes 116760
  8.6 0.0 copy-start.9
  8.6 0.7 %copy-done.9 = bf16[64,64]{1,0:T(8,128)(2,1)S(1)} copy-done((bf16[64,64]{1,0:T(8,128)(2,1)S(1)}, bf16[64,64]{1,0:T(8,128)(2,1)}, u32[]{:S(2)}) %copy-start.9) | copy-done | bytes 8216
  9.3 0.0 copy-start.11
  9.3 0.7 %copy-done.11 = f32[8,152]{1,0:T(8,128)S(1)} copy-done((f32[8,152]{1,0:T(8,128)S(1)}, f32[8,152]{1,0:T(8,128)}, u32[]{:S(2)}) %copy-start.11) | copy-done | bytes 4888
  10.0 0.0 copy-start.12
  10.0 0.7 %copy-done.12 = s32[64]{0:T(128)S(1)} copy-done((s32[64]{0:T(128)S(1)}, s32[64]{0:T(128)}, u32[]{:S(2)}) %copy-start.12) | copy-done | bytes 280
  10.7 0.0 copy-start.1
  10.7 12.2 %upward.1 = (f32[256,128]{1,0:T(8,128)}, bf16[32,256]{1,0:T(8,128)(2,1)S(1)}) custom-call(f32[3,8192]{1,0:T(4,128)S(1)} %copy-done.6, f32[3,8192]{1,0:T(4,128)S(1)} %copy-done.7, s32[64]{0:T(128)S(1)} %copy-done.12, f32[3,152,128]{2,1,0:T(8,128)S(1)} %copy-done.5, f32[8,152]{1,0:T(8,128)S(1)} %copy-done.11, bf16[64,64]{1,0:T(8,128)(2,1)S(1)} %copy-done.9, ...), custom_call_target="tpu_custom_call" | custom-call | tf_op jit(solution)/shard_map/upward/pallas_call | solution.py:370
  22.9 0.0 copy-start.10
  22.9 3.3 %collective-permute-start = (bf16[32,256]{1,0:T(8,128)(2,1)S(1)}, bf16[32,256]{1,0:T(8,128)(2,1)S(1)}, u32[]{:S(2)}, u32[]{:S(2)}) collective-permute-start(bf16[32,256]{1,0:T(8,128)(2,1)S(1)} %get-tuple-element.8), channel_id=1, source_target_pairs={{0,1},{1,0},{2,3},{3,2},{4,5},{5,4},{6,7},{7,6},{8,9},{9,8},{10,11... | collective-permute-start | bytes 49160 | tf_op jit(solution)/shard_map/ppermute | solution.py:448
  26.2 0.8 %collective-permute-done = bf16[32,256]{1,0:T(8,128)(2,1)S(1)} collective-permute-done((bf16[32,256]{1,0:T(8,128)(2,1)S(1)}, bf16[32,256]{1,0:T(8,128)(2,1)S(1)}, u32[]{:S(2)}, u32[]{:S(2)}) %collective-permute-start) | collective-permute-done | bytes 16416 | tf_op jit(solution)/shard_map/ppermute | solution.py:448
  27.0 0.0 collective-permute-start.1
  27.1 2.8 %collective-permute-done.1 = bf16[64,256]{1,0:T(8,128)(2,1)S(1)} collective-permute-done((bf16[64,256]{1,0:T(8,128)(2,1)S(1)}, bf16[64,256]{1,0:T(8,128)(2,1)S(1)}, u32[]{:S(2)}, u32[]{:S(2)}) %collective-permute-start.1) | collective-permute-done | bytes 32800 | tf_op jit(solution)/shard_map/ppermute | solution.py:448
  29.8 0.7 %collective-permute-start.2 = (bf16[128,256]{1,0:T(8,128)(2,1)S(1)}, bf16[128,256]{1,0:T(8,128)(2,1)S(1)}, u32[]{:S(2)}, u32[]{:S(2)}) collective-permute-start(bf16[128,256]{1,0:T(8,128)(2,1)S(1)} %constant_dynamic-update-slice_fusion.own), channel_id=1, source_target_pairs={{0,6},{1,7},{2,4},{3,5},{4,2},{5,3},{6,0},{7,1},{8,14},{9,15},{10,... | collective-permute-start | bytes 196616 | tf_op jit(solution)/shard_map/ppermute | solution.py:448
  30.6 13.7 %all-to-all-start = ((f32[256,1,128]{2,1,0:T(1,128)}), f32[256,1,128]{2,1,0:T(1,128)S(1)}, u32[]{:S(2)}, u32[]{:S(2)}) async-start(f32[256,1,128]{2,1,0:T(1,128)} %bitcast.3), calls=%async_computation | async-start | bytes 262144 | tf_op jit(solution)/shard_map/all_to_all | solution.py:465
  44.3 0.0 copy-start.2
  44.3 0.0 collective-permute-done.2
  44.4 1.6 %collective-permute-start.4 = (bf16[128,128]{1,0:T(8,128)(2,1)S(1)}, bf16[128,128]{1,0:T(8,128)(2,1)S(1)}, u32[]{:S(2)}, u32[]{:S(2)}) collective-permute-start(bf16[128,128]{1,0:T(8,128)(2,1)S(1)} %get-tuple-element.16), channel_id=1, source_target_pairs={{0,8},{1,9},{2,10},{3,11},{4,12},{5,13},{6,14},{7,15},{8,0},{9,1},... | collective-permute-start | bytes 98312 | tf_op jit(solution)/shard_map/ppermute | solution.py:448
  46.0 0.8 %collective-permute-start.3 = (bf16[128,128]{1,0:T(8,128)(2,1)S(1)}, bf16[128,128]{1,0:T(8,128)(2,1)S(1)}, u32[]{:S(2)}, u32[]{:S(2)}) collective-permute-start(bf16[128,128]{1,0:T(8,128)(2,1)S(1)} %get-tuple-element.17), channel_id=1, source_target_pairs={{8,16},{9,17},{10,18},{11,19},{12,20},{13,21},{14,22},{15,23},{16,... | collective-permute-start | bytes 98312 | tf_op jit(solution)/shard_map/ppermute | solution.py:459
  46.8 0.0 copy-done.1
  46.8 2.9 %operators.1.m2l = bf16[316,64,64]{2,1,0:T(8,128)(2,1)S(1)} custom-call(bf16[64,64,316]{2,1,0:T(8,128)(2,1)S(1)} %bitcast.7), custom_call_target="tpu_custom_call" | custom-call | tf_op jit(solution)/shard_map/operators/pallas_call | solution.py:392
  49.7 0.0 copy-start.3
  49.7 0.0 collective-permute-done.4
  49.7 0.0 collective-permute-done.3
  49.8 0.0 copy-done.10
  49.8 0.0 copy-done.2
  49.8 3.4 %far_field.1 = (f32[80,64]{1,0:T(8,128)S(1)}, bf16[12,64,64]{2,1,0:T(8,128)(2,1)S(1)}) custom-call(s32[8,24]{1,0:T(8,128)S(1)} %copy-done.10, bf16[128,256]{1,0:T(8,128)(2,1)S(1)} %constant_dynamic-update-slice_fusion.own, bf16[128,128]{1,0:T(8,128)(2,1)S(1)} %get-tuple-element.15.below, bf16[128,128]{1,0:T(8,128)(2,1)S(1)} %get-tuple-element.14.above, ...), custom_call_target="tpu_custom_call" | custom-call | tf_op jit(solution)/shard_map/far_field/pallas_call | solution.py:408
  53.2 4.0 %all-to-all-done = f32[256,1,128]{2,1,0:T(1,128)S(1)} async-done(((f32[256,1,128]{2,1,0:T(1,128)}), f32[256,1,128]{2,1,0:T(1,128)S(1)}, u32[]{:S(2)}, u32[]{:S(2)}) %all-to-all-start) | async-done | bytes 131104 | tf_op jit(solution)/shard_map/all_to_all | solution.py:465
  57.2 0.0 copy-done.3
  57.2 1.8 %top_levels.1 = (f32[64,73]{1,0:T(8,128)}, f32[32,64]{1,0:T(8,128)}) custom-call(s32[8,24]{1,0:T(8,128)S(1)} %copy-done.10, f32[80,64]{1,0:T(8,128)S(1)} %get-tuple-element.9.partial, bf16[12,64,64]{2,1,0:T(8,128)(2,1)S(1)} %get-tuple-element.10.device_ops, f32[256,128]{1,0:T(8,128)S(1)} %bitcast.8, bf16[63,64,64]{2,1,0:T(8,128)(2,1)S(1)} %copy-done.3), custom_call_target="tpu_custom_call" | custom-call | tf_op jit(solution)/shard_map/top_levels/pallas_call | solution.py:427
  (7 shorter events, 0.1 us)
Async XLA Ops:
  0.6 3.1 %copy-start = (f32[8,456,456]{2,1,0:T(8,128)S(1)}, f32[8,456,456]{2,1,0:T(8,128)}, u32[]{:S(2)}) copy-start(f32[8,456,456]{2,1,0:T(8,128)} %m2m_hbm.1) | copy-start | bytes 19961860
  3.8 1.2 %copy-start.4 = (f32[456,456]{1,0:T(8,128)S(1)}, f32[456,456]{1,0:T(8,128)}, u32[]{:S(2)}) copy-start(f32[456,456]{1,0:T(8,128)} %uc2ue_hbm.1) | copy-start | bytes 2495236
  4.9 0.9 %copy-start.5 = (f32[3,152,128]{2,1,0:T(8,128)S(1)}, f32[3,152,128]{2,1,0:T(8,128)}, u32[]{:S(2)}) copy-start(f32[3,152,128]{2,1,0:T(8,128)} %constant.56.clone.surface_hbm) | copy-start | bytes 700420
  5.9 0.9 %copy-start.6 = (f32[3,8192]{1,0:T(4,128)S(1)}, f32[3,8192]{1,0:T(4,128)}, u32[]{:S(2)}) copy-start(f32[3,8192]{1,0:T(4,128)} %offsets_hbm.1) | copy-start | bytes 294916
  6.8 0.9 %copy-start.7 = (f32[3,8192]{1,0:T(4,128)S(1)}, f32[3,8192]{1,0:T(4,128)}, u32[]{:S(2)}) copy-start(f32[3,8192]{1,0:T(4,128)} %forces_hbm.1) | copy-start | bytes 294916
  7.7 0.9 %copy-start.8 = (f32[456,64]{0,1:T(8,128)S(1)}, f32[456,64]{0,1:T(8,128)}, u32[]{:S(2)}) copy-start(f32[456,64]{0,1:T(8,128)} %param.18) | copy-start | bytes 350212
  8.6 0.7 %copy-start.9 = (bf16[64,64]{1,0:T(8,128)(2,1)S(1)}, bf16[64,64]{1,0:T(8,128)(2,1)}, u32[]{:S(2)}) copy-start(bf16[64,64]{1,0:T(8,128)(2,1)} %constant.58.clone.order_hbm) | copy-start | bytes 24580
  9.3 0.7 %copy-start.11 = (f32[8,152]{1,0:T(8,128)S(1)}, f32[8,152]{1,0:T(8,128)}, u32[]{:S(2)}) copy-start(f32[8,152]{1,0:T(8,128)} %constant.57.clone.points_hbm) | copy-start | bytes 14596
  10.0 0.7 %copy-start.12 = (s32[64]{0:T(128)S(1)}, s32[64]{0:T(128)}, u32[]{:S(2)}) copy-start(s32[64]{0:T(128)} %counts_hbm.1) | copy-start | bytes 772
  10.7 36.2 %copy-start.1 = (bf16[316,64,64]{0,2,1:T(8,128)(2,1)S(1)}, bf16[316,64,64]{0,2,1:T(8,128)(2,1)}, u32[]{:S(2)}) copy-start(bf16[316,64,64]{0,2,1:T(8,128)(2,1)} %param.19) | copy-start | bytes 7766020
  22.9 26.9 %copy-start.10 = (s32[8,24]{1,0:T(8,128)S(1)}, s32[8,24]{1,0:T(8,128)}, u32[]{:S(2)}) copy-start(s32[8,24]{1,0:T(8,128)} %constant.59.clone.table) | copy-start | bytes 2308
  22.9 4.2 %collective-permute-start = (bf16[32,256]{1,0:T(8,128)(2,1)S(1)}, bf16[32,256]{1,0:T(8,128)(2,1)S(1)}, u32[]{:S(2)}, u32[]{:S(2)}) collective-permute-start(bf16[32,256]{1,0:T(8,128)(2,1)S(1)} %get-tuple-element.8), channel_id=1, source_target_pairs={{0,1},{1,0},{2,3},{3,2},{4,5},{5,4},{6,7},{7,6},{8,9},{9,8},{10,11... | collective-permute-start | bytes 49160 | tf_op jit(solution)/shard_map/ppermute | solution.py:448
  27.0 2.8 %collective-permute-start.1 = (bf16[64,256]{1,0:T(8,128)(2,1)S(1)}, bf16[64,256]{1,0:T(8,128)(2,1)S(1)}, u32[]{:S(2)}, u32[]{:S(2)}) collective-permute-start(bf16[64,256]{1,0:T(8,128)(2,1)S(1)} %pad_maximum_fusion.1), channel_id=1, source_target_pairs={{0,2},{1,3},{2,0},{3,1},{4,6},{5,7},{6,4},{7,5},{8,10},{9,11},{10,... | collective-permute-start | bytes 98312 | tf_op jit(solution)/shard_map/ppermute | solution.py:448
  29.8 14.5 %collective-permute-start.2 = (bf16[128,256]{1,0:T(8,128)(2,1)S(1)}, bf16[128,256]{1,0:T(8,128)(2,1)S(1)}, u32[]{:S(2)}, u32[]{:S(2)}) collective-permute-start(bf16[128,256]{1,0:T(8,128)(2,1)S(1)} %constant_dynamic-update-slice_fusion.own), channel_id=1, source_target_pairs={{0,6},{1,7},{2,4},{3,5},{4,2},{5,3},{6,0},{7,1},{8,14},{9,15},{10,... | collective-permute-start | bytes 196616 | tf_op jit(solution)/shard_map/ppermute | solution.py:448
  30.6 26.6 %all-to-all-start = ((f32[256,1,128]{2,1,0:T(1,128)}), f32[256,1,128]{2,1,0:T(1,128)S(1)}, u32[]{:S(2)}, u32[]{:S(2)}) async-start(f32[256,1,128]{2,1,0:T(1,128)} %bitcast.3), calls=%async_computation | async-start | bytes 262144 | tf_op jit(solution)/shard_map/all_to_all | solution.py:465
  44.3 5.5 %copy-start.2 = (bf16[4,1568,128]{2,1,0:T(8,128)(2,1)S(1)}, bf16[4,1568,128]{2,1,0:T(8,128)(2,1)}, u32[]{:S(2)}) copy-start(bf16[4,1568,128]{2,1,0:T(8,128)(2,1)} %constant.60.clone.picks_hbm) | copy-start | bytes 4816900
  44.4 5.3 %collective-permute-start.4 = (bf16[128,128]{1,0:T(8,128)(2,1)S(1)}, bf16[128,128]{1,0:T(8,128)(2,1)S(1)}, u32[]{:S(2)}, u32[]{:S(2)}) collective-permute-start(bf16[128,128]{1,0:T(8,128)(2,1)S(1)} %get-tuple-element.16), channel_id=1, source_target_pairs={{0,8},{1,9},{2,10},{3,11},{4,12},{5,13},{6,14},{7,15},{8,0},{9,1},... | collective-permute-start | bytes 98312 | tf_op jit(solution)/shard_map/ppermute | solution.py:448
  46.0 3.7 %collective-permute-start.3 = (bf16[128,128]{1,0:T(8,128)(2,1)S(1)}, bf16[128,128]{1,0:T(8,128)(2,1)S(1)}, u32[]{:S(2)}, u32[]{:S(2)}) collective-permute-start(bf16[128,128]{1,0:T(8,128)(2,1)S(1)} %get-tuple-element.17), channel_id=1, source_target_pairs={{8,16},{9,17},{10,18},{11,19},{12,20},{13,21},{14,22},{15,23},{16,... | collective-permute-start | bytes 98312 | tf_op jit(solution)/shard_map/ppermute | solution.py:459
  49.7 7.5 %copy-start.3 = (bf16[63,64,64]{2,1,0:T(8,128)(2,1)S(1)}, bf16[63,64,64]{2,1,0:T(8,128)(2,1)}, u32[]{:S(2)}) copy-start(bf16[63,64,64]{2,1,0:T(8,128)(2,1)} %root_ops.1) | copy-start | bytes 1548292

commit v2 on v1

--- a/solution.py
+++ b/solution.py
@@ -19,7 +19,7 @@
 NROOT = 32
 AXIS = "morton"
 CHECK_RADIUS = 1.475
-LEAF_UNROLL = 4
+LEAF_UNROLL = 16
 
 F32 = jnp.float32
 BF16 = jnp.bfloat16
@@ -382,7 +382,7 @@
             pltpu.VMEM((LEAF_DEV, 4, NQ), F32),
             pltpu.SemaphoreType.DMA((len(operands),)),
         ],
-        compiler_params=pltpu.CompilerParams(vmem_limit_bytes=40 * 2**20),
+        compiler_params=pltpu.CompilerParams(vmem_limit_bytes=58 * 2**20),
         name="upward",
     )(*operands)
 
@@ -448,14 +448,14 @@
     return lax.ppermute(value, AXIS, [(s, s ^ mask) for s in range(devices)])
 
 
-def swapped_between(value, unit):
+def swapped_columns(value):
     devices = lax.axis_size(AXIS)
     pairs = []
     for s in range(devices):
-        b, r = divmod(s, unit)
-        t = b + 1 if b % 2 == 1 else b - 1
-        if 0 <= t < devices // unit:
-            pairs.append((s, t * unit + r))
+        column, place = divmod(s, 4)
+        other = column + 1 if column % 2 == 1 else column - 1
+        if 0 <= other < devices // 4:
+            pairs.append((s, other * 4 + (place ^ 2)))
     return lax.ppermute(value, AXIS, pairs)
 
 
@@ -465,18 +465,14 @@
     shared = lax.all_to_all(shared, AXIS, 0, 0, tiled=True)
     two = jnp.concatenate([block, swapped(block, 1)], axis=0)
     own = jnp.concatenate([two, swapped(two, 2)], axis=0)
-    pair = swapped(own, 6)
-    pair = jnp.concatenate([pair[64:], pair[:64]], axis=0)
     is_upper = me // 4 % 2 == 1
-    root_even = me // 8 % 2 == 0
-    upper_rim = jnp.where(is_upper, own[:, 128:], pair[:, 128:])
-    lower_rim = jnp.where(is_upper, pair[:, :128], own[:, :128])
-    inner = swapped(jnp.where(root_even, upper_rim, lower_rim), 8)
-    outer = swapped_between(jnp.where(root_even, lower_rim, upper_rim), 8)
-    from_below = jnp.where(root_even, outer, inner)
-    from_above = jnp.where(root_even, inner, outer)
-    below = jnp.where(is_upper, pair[:, 128:], from_below)
-    above = jnp.where(is_upper, from_above, pair[:, :128])
+    low_side, high_side = own[:, :128], own[:, 128:]
+    sibling = swapped(jnp.where(is_upper, low_side, high_side), 6)
+    further = swapped_columns(jnp.where(is_upper, high_side, low_side))
+    below = jnp.where(is_upper, sibling, further)
+    above = jnp.where(is_upper, further, sibling)
+    below = jnp.concatenate([below[64:], below[:64]], axis=0)
+    above = jnp.concatenate([above[64:], above[:64]], axis=0)
     table = jnp.asarray(device_level_table())
     partial, device_ops = far_field(table, own, below, above, operators(m2l_ops))
     return top_levels(table, partial, device_ops, shared, root_ops)

time: 59.9 us -> 52.5 us (0.88)
  local copies, waits for them, and re-layouts: 10.1 us -> 0.76 us
  Pallas kernels: 20.2 us -> 18.2 us
  starting transfers between devices: 20.2 us -> 22.2 us
  waiting for transfers between devices: 7.63 us -> 9.54 us
  other arithmetic: 0.06 us -> 0.75 us
    unnamed x28 -> x10, local copies, waits for them, and re-layouts: 10 us -> 0.74 us
    all_to_all x1, waiting for transfers between devices: 4.03 us -> 6.44 us  [body(): shared = lax.all_to_all(shared, AXIS, 0, 0, tiled=True)]
    pallas_call x1, Pallas kernels: 12.2 us -> 10.1 us  [upward(): pl.pallas_call(upward_kernel, out_shape=(jax.ShapeDtypeStruct((devices, 1...]
    ppermute x4 -> x3, starting transfers between devices: 5.67 us -> 6.96 us  [swapped(): return lax.ppermute(value, AXIS, [(s, s ^ mask) for s in range(devices)])]
    all_to_all x1, starting transfers between devices: 13.7 us -> 14.6 us  [body(): shared = lax.all_to_all(shared, AXIS, 0, 0, tiled=True)]
    concatenate x1, other arithmetic: 0.01 us -> 0.72 us  [body(): two = jnp.concatenate([block, swapped(block, 1)], axis=0)]
    ppermute x4 -> x3, waiting for transfers between devices: 3.6 us -> 3.09 us  [swapped(): return lax.ppermute(value, AXIS, [(s, s ^ mask) for s in range(devices)])]
  transfers between devices with their start and end apart: 6 -> 5, of which waited for: 3 -> 3; matrix products, arithmetic and copies ran while one was open for 0% -> 1% of each run, Pallas kernels for 11% -> 12%
where the time goes in v2:
time: 52.5 us; the launch traced here: 52.2 us
  starting transfers between devices  22.2 us (42%)
  Pallas kernels  18.2 us (35%)
  waiting for transfers between devices  9.54 us (18%)
  between operations  0.78 us (1%)
  local copies, waits for them, and re-layouts  0.76 us (1%)
  other arithmetic  0.75 us (1%)
    all_to_all x1, starting transfers between devices, body(): shared = lax.all_to_all(shared, AXIS, 0, 0, tiled=True)  14.6 us
    pallas_call x1, Pallas kernels, upward(): pl.pallas_call(upward_kernel, out_shape=(jax.ShapeDtypeStruct((devices, 1...  10.1 us
    ppermute x3, starting transfers between devices, swapped(): return lax.ppermute(value, AXIS, [(s, s ^ mask) for s in range(devices)])  6.96 us
    all_to_all x1, waiting for transfers between devices, body(): shared = lax.all_to_all(shared, AXIS, 0, 0, tiled=True)  6.44 us
    pallas_call x1, Pallas kernels, far_field(): pl.pallas_call(far_kernel, out_shape=(jax.ShapeDtypeStruct((80, RANK), F3...  3.35 us
    ppermute x3, waiting for transfers between devices, swapped(): return lax.ppermute(value, AXIS, [(s, s ^ mask) for s in range(devices)])  3.09 us
    pallas_call x1, Pallas kernels, operators(): pl.pallas_call(operators_kernel, out_shape=jax.ShapeDtypeStruct(m2l_ops.s...  2.85 us
    pallas_call x1, Pallas kernels, top_levels(): pl.pallas_call(top_kernel, out_shape=(jax.ShapeDtypeStruct((RANK, BOX_DEV...  1.8 us
  transfers between devices with their start and end apart: 5, of which 3 were waited for; matrix products, arithmetic and copies ran while one was open for 1% of the time, Pallas kernels for 12%

profile of v2, /device:TPU:1, one launch (start us, length us, event | category | flops | bytes accessed | tf_op | source)
XLA Modules:
  0.0 52.2 jit_solution(8708963667000305611)
XLA Ops:
  0.6 0.0 copy-start
  0.6 10.1 %upward.1 = (f32[256,128]{1,0:T(8,128)}, bf16[32,256]{1,0:T(8,128)(2,1)}) custom-call(f32[3,8192]{1,0:T(4,128)} %offsets_hbm.1, f32[3,8192]{1,0:T(4,128)} %forces_hbm.1, s32[64]{0:T(128)} %counts_hbm.1, f32[3,152,128]{2,1,0:T(8,128)} %constant.41.clone.surface_hbm, f32[8,152]{1,0:T(8,128)} %constant.42.clone.points_hbm, ...), custom_call_target="tpu_custom_call" | custom-call | tf_op jit(solution)/shard_map/upward/pallas_call | solution.py:370
  10.8 0.0 copy-start.3
  10.8 3.3 %collective-permute-start = (bf16[32,256]{1,0:T(8,128)(2,1)}, bf16[32,256]{1,0:T(8,128)(2,1)S(1)}, u32[]{:S(2)}, u32[]{:S(2)}) collective-permute-start(bf16[32,256]{1,0:T(8,128)(2,1)} %get-tuple-element.8), channel_id=1, source_target_pairs={{0,1},{1,0},{2,3},{3,2},{4,5},{5,4},{6,7},{7,6},{8,9},{9,8},{10,11... | collective-permute-start | bytes 49160 | tf_op jit(solution)/shard_map/ppermute | solution.py:448
  14.1 0.7 %constant_dynamic-update-slice_fusion.2 = bf16[128,256]{1,0:T(8,128)(2,1)S(1)} fusion(bf16[32,256]{1,0:T(8,128)(2,1)} %get-tuple-element.8), kind=kLoop, calls=%fused_computation.9 | loop fusion | bytes 32768
  14.9 0.3 collective-permute-done
  15.2 0.7 %pad_maximum_fusion = bf16[64,256]{1,0:T(8,128)(2,1)S(1)} fusion(bf16[32,256]{1,0:T(8,128)(2,1)S(1)} %collective-permute-done, bf16[32,256]{1,0:T(8,128)(2,1)} %get-tuple-element.8), kind=kLoop, calls=%fused_computation | loop fusion | flops 65536 | bytes 65536 | tf_op jit(solution)/shard_map/concatenate | solution.py:466
  15.9 0.0 collective-permute-start.1
  15.9 2.8 %collective-permute-done.1 = bf16[64,256]{1,0:T(8,128)(2,1)S(1)} collective-permute-done((bf16[64,256]{1,0:T(8,128)(2,1)S(1)}, bf16[64,256]{1,0:T(8,128)(2,1)S(1)}, u32[]{:S(2)}, u32[]{:S(2)}) %collective-permute-start.1) | collective-permute-done | bytes 32800 | tf_op jit(solution)/shard_map/ppermute | solution.py:448
  18.7 0.7 %collective-permute-start.3 = (bf16[128,128]{1,0:T(8,128)(2,1)S(1)}, bf16[128,128]{1,0:T(8,128)(2,1)S(1)}, u32[]{:S(2)}, u32[]{:S(2)}) collective-permute-start(bf16[128,128]{1,0:T(8,128)(2,1)S(1)} %get-tuple-element.16), channel_id=1, source_target_pairs={{4,10},{5,11},{6,8},{7,9},{8,6},{9,7},{10,4},{11,5},{12,18},{13,19... | collective-permute-start | bytes 98312 | tf_op jit(solution)/shard_map/ppermute | solution.py:459
  19.4 3.6 %collective-permute-start.2 = (bf16[128,128]{1,0:T(8,128)(2,1)S(1)}, bf16[128,128]{1,0:T(8,128)(2,1)S(1)}, u32[]{:S(2)}, u32[]{:S(2)}) collective-permute-start(bf16[128,128]{1,0:T(8,128)(2,1)S(1)} %get-tuple-element.17), channel_id=1, source_target_pairs={{0,6},{1,7},{2,4},{3,5},{4,2},{5,3},{6,0},{7,1},{8,14},{9,15},{10,... | collective-permute-start | bytes 98312 | tf_op jit(solution)/shard_map/ppermute | solution.py:448
  23.0 14.6 %all-to-all-start = ((f32[256,1,128]{2,1,0:T(1,128)}), f32[256,1,128]{2,1,0:T(1,128)S(1)}, u32[]{:S(2)}, u32[]{:S(2)}) async-start(f32[256,1,128]{2,1,0:T(1,128)} %bitcast.10), calls=%async_computation | async-start | bytes 262144 | tf_op jit(solution)/shard_map/all_to_all | solution.py:465
  37.6 0.0 copy-start.1
  37.6 0.0 copy-done
  37.6 2.9 %operators.1.m2l = bf16[316,64,64]{2,1,0:T(8,128)(2,1)S(1)} custom-call(bf16[64,64,316]{2,1,0:T(8,128)(2,1)S(1)} %bitcast.7), custom_call_target="tpu_custom_call" | custom-call | tf_op jit(solution)/shard_map/operators/pallas_call | solution.py:392
  40.5 0.0 copy-start.2
  40.5 0.0 collective-permute-done.3
  40.5 0.0 collective-permute-done.2
  40.6 0.0 copy-done.3
  40.6 0.0 copy-done.1
  40.6 3.4 %far_field.1 = (f32[80,64]{1,0:T(8,128)S(1)}, bf16[12,64,64]{2,1,0:T(8,128)(2,1)S(1)}) custom-call(s32[8,24]{1,0:T(8,128)S(1)} %copy-done.3, bf16[128,256]{1,0:T(8,128)(2,1)S(1)} %constant_dynamic-update-slice_fusion.own, bf16[128,128]{1,0:T(8,128)(2,1)S(1)} %pad_maximum_fusion.1.below, bf16[128,128]{1,0:T(8,128)(2,1)S(1)} %pad_maximum_fusion.2.above, ...), custom_call_target="tpu_custom_call" | custom-call | tf_op jit(solution)/shard_map/far_field/pallas_call | solution.py:408
  43.9 6.4 %all-to-all-done = f32[256,1,128]{2,1,0:T(1,128)S(1)} async-done(((f32[256,1,128]{2,1,0:T(1,128)}), f32[256,1,128]{2,1,0:T(1,128)S(1)}, u32[]{:S(2)}, u32[]{:S(2)}) %all-to-all-start) | async-done | bytes 131104 | tf_op jit(solution)/shard_map/all_to_all | solution.py:465
  50.4 0.0 copy-done.2
  50.4 1.8 %top_levels.1 = (f32[64,73]{1,0:T(8,128)}, f32[32,64]{1,0:T(8,128)}) custom-call(s32[8,24]{1,0:T(8,128)S(1)} %copy-done.3, f32[80,64]{1,0:T(8,128)S(1)} %get-tuple-element.9.partial, bf16[12,64,64]{2,1,0:T(8,128)(2,1)S(1)} %get-tuple-element.10.device_ops, f32[256,128]{1,0:T(8,128)S(1)} %bitcast.8, bf16[63,64,64]{2,1,0:T(8,128)(2,1)S(1)} %copy-done.2), custom_call_target="tpu_custom_call" | custom-call | tf_op jit(solution)/shard_map/top_levels/pallas_call | solution.py:427
  (7 shorter events, 0.0 us)
Async XLA Ops:
  0.6 37.0 %copy-start = (bf16[316,64,64]{0,2,1:T(8,128)(2,1)S(1)}, bf16[316,64,64]{0,2,1:T(8,128)(2,1)}, u32[]{:S(2)}) copy-start(bf16[316,64,64]{0,2,1:T(8,128)(2,1)} %param.19) | copy-start | bytes 7766020
  10.8 29.8 %copy-start.3 = (s32[8,24]{1,0:T(8,128)S(1)}, s32[8,24]{1,0:T(8,128)}, u32[]{:S(2)}) copy-start(s32[8,24]{1,0:T(8,128)} %constant.44.clone.table) | copy-start | bytes 2308
  10.8 4.4 %collective-permute-start = (bf16[32,256]{1,0:T(8,128)(2,1)}, bf16[32,256]{1,0:T(8,128)(2,1)S(1)}, u32[]{:S(2)}, u32[]{:S(2)}) collective-permute-start(bf16[32,256]{1,0:T(8,128)(2,1)} %get-tuple-element.8), channel_id=1, source_target_pairs={{0,1},{1,0},{2,3},{3,2},{4,5},{5,4},{6,7},{7,6},{8,9},{9,8},{10,11... | collective-permute-start | bytes 49160 | tf_op jit(solution)/shard_map/ppermute | solution.py:448
  15.9 2.8 %collective-permute-start.1 = (bf16[64,256]{1,0:T(8,128)(2,1)S(1)}, bf16[64,256]{1,0:T(8,128)(2,1)S(1)}, u32[]{:S(2)}, u32[]{:S(2)}) collective-permute-start(bf16[64,256]{1,0:T(8,128)(2,1)S(1)} %pad_maximum_fusion), channel_id=1, source_target_pairs={{0,2},{1,3},{2,0},{3,1},{4,6},{5,7},{6,4},{7,5},{8,10},{9,11},{10,... | collective-permute-start | bytes 98312 | tf_op jit(solution)/shard_map/ppermute | solution.py:448
  18.7 21.8 %collective-permute-start.3 = (bf16[128,128]{1,0:T(8,128)(2,1)S(1)}, bf16[128,128]{1,0:T(8,128)(2,1)S(1)}, u32[]{:S(2)}, u32[]{:S(2)}) collective-permute-start(bf16[128,128]{1,0:T(8,128)(2,1)S(1)} %get-tuple-element.16), channel_id=1, source_target_pairs={{4,10},{5,11},{6,8},{7,9},{8,6},{9,7},{10,4},{11,5},{12,18},{13,19... | collective-permute-start | bytes 98312 | tf_op jit(solution)/shard_map/ppermute | solution.py:459
  19.4 21.1 %collective-permute-start.2 = (bf16[128,128]{1,0:T(8,128)(2,1)S(1)}, bf16[128,128]{1,0:T(8,128)(2,1)S(1)}, u32[]{:S(2)}, u32[]{:S(2)}) collective-permute-start(bf16[128,128]{1,0:T(8,128)(2,1)S(1)} %get-tuple-element.17), channel_id=1, source_target_pairs={{0,6},{1,7},{2,4},{3,5},{4,2},{5,3},{6,0},{7,1},{8,14},{9,15},{10,... | collective-permute-start | bytes 98312 | tf_op jit(solution)/shard_map/ppermute | solution.py:448
  23.0 27.4 %all-to-all-start = ((f32[256,1,128]{2,1,0:T(1,128)}), f32[256,1,128]{2,1,0:T(1,128)S(1)}, u32[]{:S(2)}, u32[]{:S(2)}) async-start(f32[256,1,128]{2,1,0:T(1,128)} %bitcast.10), calls=%async_computation | async-start | bytes 262144 | tf_op jit(solution)/shard_map/all_to_all | solution.py:465
  37.6 3.0 %copy-start.1 = (bf16[4,1568,128]{2,1,0:T(8,128)(2,1)S(1)}, bf16[4,1568,128]{2,1,0:T(8,128)(2,1)}, u32[]{:S(2)}) copy-start(bf16[4,1568,128]{2,1,0:T(8,128)(2,1)} %constant.45.clone.picks_hbm) | copy-start | bytes 4816900
  40.5 9.9 %copy-start.2 = (bf16[63,64,64]{2,1,0:T(8,128)(2,1)S(1)}, bf16[63,64,64]{2,1,0:T(8,128)(2,1)}, u32[]{:S(2)}) copy-start(bf16[63,64,64]{2,1,0:T(8,128)(2,1)} %root_ops.1) | copy-start | bytes 1548292

commit v3 on v2

--- a/solution.py
+++ b/solution.py
@@ -365,13 +365,14 @@
         offsets, forces, counts, jnp.asarray(spread), jnp.asarray(rows), jnp.asarray(leaf_order()),
         uc2ue, m2m_ops, compress.T,
     )
+    operands = tuple(pltpu.with_memory_space_constraint(x, pltpu.HBM) for x in operands)
     held = [pltpu.VMEM(x.shape, x.dtype) for x in operands]
     held[2] = pltpu.SMEM(counts.shape, counts.dtype)
     return pl.pallas_call(
         upward_kernel,
         out_shape=(
-            jax.ShapeDtypeStruct((devices, 128), F32),
-            jax.ShapeDtypeStruct((32, 256), BF16),
+            pltpu.VMEM((devices, 128), F32),
+            pltpu.VMEM((32, 256), BF16),
         ),
         in_specs=[whole(pltpu.HBM)] * len(operands),
         out_specs=(whole(), whole()),
@@ -382,7 +383,7 @@
             pltpu.VMEM((LEAF_DEV, 4, NQ), F32),
             pltpu.SemaphoreType.DMA((len(operands),)),
         ],
-        compiler_params=pltpu.CompilerParams(vmem_limit_bytes=58 * 2**20),
+        compiler_params=pltpu.CompilerParams(vmem_limit_bytes=40 * 2**20),
         name="upward",
     )(*operands)
 

time: 52.5 us -> 51.4 us (0.979)
  other arithmetic: 0.75 us -> 0.03 us
  local copies, waits for them, and re-layouts: 0.76 us -> 0.04 us
    concatenate x1, other arithmetic: 0.72 us -> 0.01 us  [body(): two = jnp.concatenate([block, swapped(block, 1)], axis=0)]
    unnamed x10, local copies, waits for them, and re-layouts: 0.74 us -> 0.03 us
  transfers between devices with their start and end apart: 5 -> 5, of which waited for: 3 -> 3; matrix products, arithmetic and copies ran while one was open for 1% -> 0% of each run, Pallas kernels for 12% -> 12%
where the time goes in v3:
time: 51.4 us; the launch traced here: 51.3 us
  starting transfers between devices  22.2 us (43%)
  Pallas kernels  18.1 us (35%)
  waiting for transfers between devices  10 us (19%)
  between operations  0.78 us (2%)
    all_to_all x1, starting transfers between devices, body(): shared = lax.all_to_all(shared, AXIS, 0, 0, tiled=True)  14.6 us
    pallas_call x1, Pallas kernels, upward(): pl.pallas_call(upward_kernel, out_shape=(pltpu.VMEM((devices, 128), F32),...  10.1 us
    ppermute x3, starting transfers between devices, swapped(): return lax.ppermute(value, AXIS, [(s, s ^ mask) for s in range(devices)])  6.96 us
    all_to_all x1, waiting for transfers between devices, body(): shared = lax.all_to_all(shared, AXIS, 0, 0, tiled=True)  6.43 us
    ppermute x3, waiting for transfers between devices, swapped(): return lax.ppermute(value, AXIS, [(s, s ^ mask) for s in range(devices)])  3.6 us
    pallas_call x1, Pallas kernels, far_field(): pl.pallas_call(far_kernel, out_shape=(jax.ShapeDtypeStruct((80, RANK), F3...  3.36 us
    pallas_call x1, Pallas kernels, operators(): pl.pallas_call(operators_kernel, out_shape=jax.ShapeDtypeStruct(m2l_ops.s...  2.85 us
    pallas_call x1, Pallas kernels, top_levels(): pl.pallas_call(top_kernel, out_shape=(jax.ShapeDtypeStruct((RANK, BOX_DEV...  1.8 us
  transfers between devices with their start and end apart: 5, of which 3 were waited for; matrix products, arithmetic and copies ran while one was open for 0% of the time, Pallas kernels for 12%

profile of v3, /device:TPU:1, one launch (start us, length us, event | category | flops | bytes accessed | tf_op | source)
XLA Modules:
  0.0 51.3 jit_solution(11491236108538345988)
XLA Ops:
  0.6 0.0 copy-start
  0.6 10.1 %upward.1 = (f32[256,128]{1,0:T(8,128)}, bf16[32,256]{1,0:T(8,128)(2,1)S(1)}) custom-call(f32[3,8192]{1,0:T(4,128)} %offsets_hbm.1, f32[3,8192]{1,0:T(4,128)} %forces_hbm.1, s32[64]{0:T(128)} %counts_hbm.1, f32[3,152,128]{2,1,0:T(8,128)} %constant.41.clone.surface_hbm, f32[8,152]{1,0:T(8,128)} %constant.42.clone.points_hbm, ...), custom_call_target="tpu_custom_call" | custom-call | tf_op jit(solution)/shard_map/upward/pallas_call | solution.py:371
  10.8 0.0 copy-start.3
  10.8 3.3 %collective-permute-start = (bf16[32,256]{1,0:T(8,128)(2,1)S(1)}, bf16[32,256]{1,0:T(8,128)(2,1)S(1)}, u32[]{:S(2)}, u32[]{:S(2)}) collective-permute-start(bf16[32,256]{1,0:T(8,128)(2,1)S(1)} %get-tuple-element.8), channel_id=1, source_target_pairs={{0,1},{1,0},{2,3},{3,2},{4,5},{5,4},{6,7},{7,6},{8,9},{9,8},{10,11... | collective-permute-start | bytes 49160 | tf_op jit(solution)/shard_map/ppermute | solution.py:449
  14.1 0.8 %collective-permute-done = bf16[32,256]{1,0:T(8,128)(2,1)S(1)} collective-permute-done((bf16[32,256]{1,0:T(8,128)(2,1)S(1)}, bf16[32,256]{1,0:T(8,128)(2,1)S(1)}, u32[]{:S(2)}, u32[]{:S(2)}) %collective-permute-start) | collective-permute-done | bytes 16416 | tf_op jit(solution)/shard_map/ppermute | solution.py:449
  15.0 0.0 collective-permute-start.1
  15.0 2.8 %collective-permute-done.1 = bf16[64,256]{1,0:T(8,128)(2,1)S(1)} collective-permute-done((bf16[64,256]{1,0:T(8,128)(2,1)S(1)}, bf16[64,256]{1,0:T(8,128)(2,1)S(1)}, u32[]{:S(2)}, u32[]{:S(2)}) %collective-permute-start.1) | collective-permute-done | bytes 32800 | tf_op jit(solution)/shard_map/ppermute | solution.py:449
  17.8 0.7 %collective-permute-start.3 = (bf16[128,128]{1,0:T(8,128)(2,1)S(1)}, bf16[128,128]{1,0:T(8,128)(2,1)S(1)}, u32[]{:S(2)}, u32[]{:S(2)}) collective-permute-start(bf16[128,128]{1,0:T(8,128)(2,1)S(1)} %get-tuple-element.16), channel_id=1, source_target_pairs={{4,10},{5,11},{6,8},{7,9},{8,6},{9,7},{10,4},{11,5},{12,18},{13,19... | collective-permute-start | bytes 98312 | tf_op jit(solution)/shard_map/ppermute | solution.py:460
  18.4 3.6 %collective-permute-start.2 = (bf16[128,128]{1,0:T(8,128)(2,1)S(1)}, bf16[128,128]{1,0:T(8,128)(2,1)S(1)}, u32[]{:S(2)}, u32[]{:S(2)}) collective-permute-start(bf16[128,128]{1,0:T(8,128)(2,1)S(1)} %get-tuple-element.17), channel_id=1, source_target_pairs={{0,6},{1,7},{2,4},{3,5},{4,2},{5,3},{6,0},{7,1},{8,14},{9,15},{10,... | collective-permute-start | bytes 98312 | tf_op jit(solution)/shard_map/ppermute | solution.py:449
  22.1 14.6 %all-to-all-start = ((f32[256,1,128]{2,1,0:T(1,128)}), f32[256,1,128]{2,1,0:T(1,128)S(1)}, u32[]{:S(2)}, u32[]{:S(2)}) async-start(f32[256,1,128]{2,1,0:T(1,128)} %bitcast.3), calls=%async_computation | async-start | bytes 262144 | tf_op jit(solution)/shard_map/all_to_all | solution.py:466
  36.7 0.0 copy-start.1
  36.7 0.0 copy-done
  36.7 2.9 %operators.1.m2l = bf16[316,64,64]{2,1,0:T(8,128)(2,1)S(1)} custom-call(bf16[64,64,316]{2,1,0:T(8,128)(2,1)S(1)} %bitcast.7), custom_call_target="tpu_custom_call" | custom-call | tf_op jit(solution)/shard_map/operators/pallas_call | solution.py:393
  39.5 0.0 copy-start.2
  39.5 0.0 collective-permute-done.3
  39.6 0.0 collective-permute-done.2
  39.6 0.0 copy-done.3
  39.6 0.0 copy-done.1
  39.6 3.4 %far_field.1 = (f32[80,64]{1,0:T(8,128)S(1)}, bf16[12,64,64]{2,1,0:T(8,128)(2,1)S(1)}) custom-call(s32[8,24]{1,0:T(8,128)S(1)} %copy-done.3, bf16[128,256]{1,0:T(8,128)(2,1)S(1)} %constant_dynamic-update-slice_fusion.own, bf16[128,128]{1,0:T(8,128)(2,1)S(1)} %pad_maximum_fusion.1.below, bf16[128,128]{1,0:T(8,128)(2,1)S(1)} %pad_maximum_fusion.2.above, ...), custom_call_target="tpu_custom_call" | custom-call | tf_op jit(solution)/shard_map/far_field/pallas_call | solution.py:409
  43.0 6.4 %all-to-all-done = f32[256,1,128]{2,1,0:T(1,128)S(1)} async-done(((f32[256,1,128]{2,1,0:T(1,128)}), f32[256,1,128]{2,1,0:T(1,128)S(1)}, u32[]{:S(2)}, u32[]{:S(2)}) %all-to-all-start) | async-done | bytes 131104 | tf_op jit(solution)/shard_map/all_to_all | solution.py:466
  49.5 0.0 copy-done.2
  49.5 1.8 %top_levels.1 = (f32[64,73]{1,0:T(8,128)}, f32[32,64]{1,0:T(8,128)}) custom-call(s32[8,24]{1,0:T(8,128)S(1)} %copy-done.3, f32[80,64]{1,0:T(8,128)S(1)} %get-tuple-element.9.partial, bf16[12,64,64]{2,1,0:T(8,128)(2,1)S(1)} %get-tuple-element.10.device_ops, f32[256,128]{1,0:T(8,128)S(1)} %bitcast.8, bf16[63,64,64]{2,1,0:T(8,128)(2,1)S(1)} %copy-done.2), custom_call_target="tpu_custom_call" | custom-call | tf_op jit(solution)/shard_map/top_levels/pallas_call | solution.py:428
  (9 shorter events, 0.0 us)
Async XLA Ops:
  0.6 36.0 %copy-start = (bf16[316,64,64]{0,2,1:T(8,128)(2,1)S(1)}, bf16[316,64,64]{0,2,1:T(8,128)(2,1)}, u32[]{:S(2)}) copy-start(bf16[316,64,64]{0,2,1:T(8,128)(2,1)} %param.19) | copy-start | bytes 7766020
  10.8 28.8 %copy-start.3 = (s32[8,24]{1,0:T(8,128)S(1)}, s32[8,24]{1,0:T(8,128)}, u32[]{:S(2)}) copy-start(s32[8,24]{1,0:T(8,128)} %constant.44.clone.table) | copy-start | bytes 2308
  10.8 4.2 %collective-permute-start = (bf16[32,256]{1,0:T(8,128)(2,1)S(1)}, bf16[32,256]{1,0:T(8,128)(2,1)S(1)}, u32[]{:S(2)}, u32[]{:S(2)}) collective-permute-start(bf16[32,256]{1,0:T(8,128)(2,1)S(1)} %get-tuple-element.8), channel_id=1, source_target_pairs={{0,1},{1,0},{2,3},{3,2},{4,5},{5,4},{6,7},{7,6},{8,9},{9,8},{10,11... | collective-permute-start | bytes 49160 | tf_op jit(solution)/shard_map/ppermute | solution.py:449
  15.0 2.8 %collective-permute-start.1 = (bf16[64,256]{1,0:T(8,128)(2,1)S(1)}, bf16[64,256]{1,0:T(8,128)(2,1)S(1)}, u32[]{:S(2)}, u32[]{:S(2)}) collective-permute-start(bf16[64,256]{1,0:T(8,128)(2,1)S(1)} %pad_maximum_fusion), channel_id=1, source_target_pairs={{0,2},{1,3},{2,0},{3,1},{4,6},{5,7},{6,4},{7,5},{8,10},{9,11},{10,... | collective-permute-start | bytes 98312 | tf_op jit(solution)/shard_map/ppermute | solution.py:449
  17.8 21.8 %collective-permute-start.3 = (bf16[128,128]{1,0:T(8,128)(2,1)S(1)}, bf16[128,128]{1,0:T(8,128)(2,1)S(1)}, u32[]{:S(2)}, u32[]{:S(2)}) collective-permute-start(bf16[128,128]{1,0:T(8,128)(2,1)S(1)} %get-tuple-element.16), channel_id=1, source_target_pairs={{4,10},{5,11},{6,8},{7,9},{8,6},{9,7},{10,4},{11,5},{12,18},{13,19... | collective-permute-start | bytes 98312 | tf_op jit(solution)/shard_map/ppermute | solution.py:460
  18.4 21.1 %collective-permute-start.2 = (bf16[128,128]{1,0:T(8,128)(2,1)S(1)}, bf16[128,128]{1,0:T(8,128)(2,1)S(1)}, u32[]{:S(2)}, u32[]{:S(2)}) collective-permute-start(bf16[128,128]{1,0:T(8,128)(2,1)S(1)} %get-tuple-element.17), channel_id=1, source_target_pairs={{0,6},{1,7},{2,4},{3,5},{4,2},{5,3},{6,0},{7,1},{8,14},{9,15},{10,... | collective-permute-start | bytes 98312 | tf_op jit(solution)/shard_map/ppermute | solution.py:449
  22.1 27.4 %all-to-all-start = ((f32[256,1,128]{2,1,0:T(1,128)}), f32[256,1,128]{2,1,0:T(1,128)S(1)}, u32[]{:S(2)}, u32[]{:S(2)}) async-start(f32[256,1,128]{2,1,0:T(1,128)} %bitcast.3), calls=%async_computation | async-start | bytes 262144 | tf_op jit(solution)/shard_map/all_to_all | solution.py:466
  36.7 3.0 %copy-start.1 = (bf16[4,1568,128]{2,1,0:T(8,128)(2,1)S(1)}, bf16[4,1568,128]{2,1,0:T(8,128)(2,1)}, u32[]{:S(2)}) copy-start(bf16[4,1568,128]{2,1,0:T(8,128)(2,1)} %constant.45.clone.picks_hbm) | copy-start | bytes 4816900
  39.5 9.9 %copy-start.2 = (bf16[63,64,64]{2,1,0:T(8,128)(2,1)S(1)}, bf16[63,64,64]{2,1,0:T(8,128)(2,1)}, u32[]{:S(2)}) copy-start(bf16[63,64,64]{2,1,0:T(8,128)(2,1)} %root_ops.1) | copy-start | bytes 1548292

commit v4 on v3

--- a/solution.py
+++ b/solution.py
@@ -19,7 +19,7 @@
 NROOT = 32
 AXIS = "morton"
 CHECK_RADIUS = 1.475
-LEAF_UNROLL = 16
+LEAF_UNROLL = 64
 
 F32 = jnp.float32
 BF16 = jnp.bfloat16
@@ -99,13 +99,13 @@
 
 
 def split(x):
+    high = x.astype(BF16)
+    return high, (x - high.astype(F32)).astype(BF16)
+
+
+def stacked(x):
     high = x.astype(BF16).astype(F32)
-    return high, x - high
-
-
-def stacked(x):
-    high, low = split(x)
-    return jnp.concatenate([high, low], axis=0).astype(BF16)
+    return jnp.concatenate([high, x - high], axis=0).astype(BF16)
 
 
 def dot(a, b):
@@ -159,8 +159,8 @@
             [jnp.concatenate([f, zero], axis=0), jnp.concatenate([-u, one], axis=0)], axis=1
         )
         left = stacked(left)
-        top = dot_nt(left, high.astype(BF16))
-        rest = dot_nt(left, low.astype(BF16))
+        top = dot_nt(left, high)
+        rest = dot_nt(left, low)
         sums = top[0:4] + (top[4:8] + rest[0:4])
         octant = (l >> 4 & 1) * 4 + (l >> 2 & 1) * 2 + (l & 1)
         parent = (l >> 5 & 1) * 4 + (l >> 3 & 1) * 2 + (l >> 1 & 1)
@@ -175,11 +175,10 @@
     for s in range(3):
         rows = check[:, s, :] + check[:, 3, :] * points[s : s + 1, :]
         w_high, w_low = split(uc2ue[s * NQ : (s + 1) * NQ, :])
-        density = density + product(rows, w_high.astype(BF16), w_low.astype(BF16))
+        density = density + product(rows, w_high, w_low)
     shrink = compress[...]
     shrink = jnp.concatenate([shrink, shrink], axis=0)
     s_high, s_low = split(shrink)
-    s_high, s_low = s_high.astype(BF16), s_low.astype(BF16)
     lower = lax.broadcasted_iota(jnp.int32, (1, 128), 1) < RANK
     leaves = product(density, s_high, s_low, dot_nt).astype(BF16)
     leaves = dot(order[...], leaves)
@@ -190,7 +189,6 @@
     parents = jnp.zeros((8, NCOEF), F32)
     for o in range(8):
         w_high, w_low = split(m2m[o])
-        w_high, w_low = w_high.astype(BF16), w_low.astype(BF16)
         m2m_high[o] = w_high
         m2m_low[o] = w_low
         parents = parents + product(density[o * 8 : o * 8 + 8], w_high, w_low)
@@ -198,7 +196,7 @@
     middle = jnp.where(lower, middle[0:4], middle[4:8])
 
     def one_row(x, w_high, w_low, dot=dot):
-        high, low = split(x)
+        high, low = (part.astype(F32) for part in split(x))
         row = lax.broadcasted_iota(jnp.int32, (8, 1), 0)
         both = jnp.where(row == 0, high, jnp.where(row == 1, low, 0.0)).astype(BF16)
         top = dot(both, w_high)
@@ -218,7 +216,7 @@
     block[16:32, 128:256] = middle
 
 
-def operators_kernel(source_hbm, out, source, turned, sem):
+def operators_kernel(source_hbm, out_hbm, source, turned, out, sem, out_sems):
     fetch = pltpu.make_async_copy(source_hbm, source, sem)
     fetch.start()
     directions = source.shape[2]
@@ -233,21 +231,37 @@
         moved = dot_nt(unit, four)
         for half in range(2):
             turned[half, g * pitch : g * pitch + rows, :] = moved[:, half * 128 : half * 128 + 128]
+    part_size, all_leaving = (directions + 3) // 4, []
     for d in range(directions):
         parts = []
         for half in range(2):
             pair = turned[half, pl.ds(d, 16, stride=pitch), :]
             parts += [pair, pltpu.roll(pair, RANK, 1)]
         out[d] = jnp.concatenate(parts, axis=0)[:, :RANK].astype(BF16)
-
-
-def far_kernel(table, own, below, above, picks_hbm, m2l, boxes, device_ops, picks, near, sem):
+        if (d + 1) % part_size == 0 or d + 1 == directions:
+            chunk = d // part_size
+            first = chunk * part_size
+            leaving = pltpu.make_async_copy(
+                out.at[first : d + 1], out_hbm.at[first : d + 1], out_sems.at[chunk]
+            )
+            leaving.start()
+            all_leaving.append(leaving)
+    for leaving in all_leaving:
+        leaving.wait()
+
+
+def far_kernel(
+    table, own, below, above, picks_hbm, m2l_hbm, root_hbm, boxes, device_ops, root_ops,
+    picks, near, m2l, sem, m2l_sem, root_sem,
+):
     me = lax.axis_index(AXIS)
     fetch = pltpu.make_async_copy(picks_hbm.at[me % 4], picks, sem)
     fetch.start()
+    fetch_m2l = pltpu.make_async_copy(m2l_hbm, m2l, m2l_sem)
+    fetch_m2l.start()
+    fetch_root = pltpu.make_async_copy(root_hbm, root_ops, root_sem)
+    fetch_root.start()
     lower = lax.broadcasted_iota(jnp.int32, (1, 128), 1) < RANK
-    for n in range(12):
-        device_ops[n] = m2l[table[me % 8, n]]
 
     x01, x23, x45, x67 = below[...], own[:, 0:128], own[:, 128:256], above[...]
 
@@ -279,6 +293,9 @@
     level1_far = ((7, 3), (0, 10))
     first_rows = lax.broadcasted_iota(jnp.int32, (16, 128), 0) < 4
     total = jnp.zeros((80, RANK), F32)
+    fetch_m2l.wait()
+    for n in range(12):
+        device_ops[n] = m2l[table[me % 8, n]]
     for pair in range(49):
         v, w = pair // 7 - 3, pair % 7 - 3
         close = max(abs(v), abs(w)) < 2
@@ -298,6 +315,7 @@
         if not close:
             left = left[:, : 7 * RANK]
         total = total + dot(left, jnp.concatenate(operator, axis=0))
+    fetch_root.wait()
     boxes[...] = jnp.zeros(boxes.shape, F32)
     boxes[1:9, :] = total[64:72]
     for p in range(2):
@@ -392,36 +410,44 @@
     count = m2l_ops.shape[0]
     return pl.pallas_call(
         operators_kernel,
-        out_shape=jax.ShapeDtypeStruct(m2l_ops.shape, BF16),
+        out_shape=pltpu.HBM(m2l_ops.shape, BF16),
         in_specs=[whole(pltpu.HBM)],
-        out_specs=whole(),
+        out_specs=whole(pltpu.HBM),
         scratch_shapes=[
             pltpu.VMEM((RANK, RANK, count), BF16),
             pltpu.VMEM((2, 16 * (count + 5), 128), F32),
+            pltpu.VMEM(m2l_ops.shape, BF16),
             pltpu.SemaphoreType.DMA,
+            pltpu.SemaphoreType.DMA((4,)),
         ],
         compiler_params=pltpu.CompilerParams(vmem_limit_bytes=28 * 2**20),
         name="operators",
     )(jnp.transpose(m2l_ops, (1, 2, 0)))
 
 
-def far_field(table, own, below, above, m2l):
+def far_field(table, own, below, above, m2l, root_ops):
+    held = (jnp.asarray(cross_section_picks()), m2l, root_ops)
+    held = [pltpu.with_memory_space_constraint(x, pltpu.HBM) for x in held]
     return pl.pallas_call(
         far_kernel,
         out_shape=(
             jax.ShapeDtypeStruct((80, RANK), F32),
             jax.ShapeDtypeStruct((12, RANK, RANK), BF16),
+            jax.ShapeDtypeStruct(root_ops.shape, BF16),
         ),
-        in_specs=[whole(pltpu.SMEM), whole(), whole(), whole(), whole(pltpu.HBM), whole()],
-        out_specs=(whole(), whole()),
+        in_specs=[whole(pltpu.SMEM), whole(), whole(), whole()] + [whole(pltpu.HBM)] * 3,
+        out_specs=(whole(),) * 3,
         scratch_shapes=[
             pltpu.VMEM((49 * 32, 128), BF16),
             pltpu.VMEM((49 * 32, 11 * 128), BF16),
+            pltpu.VMEM(m2l.shape, BF16),
+            pltpu.SemaphoreType.DMA,
+            pltpu.SemaphoreType.DMA,
             pltpu.SemaphoreType.DMA,
         ],
         compiler_params=pltpu.CompilerParams(vmem_limit_bytes=28 * 2**20),
         name="far_field",
-    )(table, own, below, above, jnp.asarray(cross_section_picks()), m2l)
+    )(table, own, below, above, *held)
 
 
 def top_levels(table, partial, device_ops, shared, root_ops):
@@ -466,6 +492,7 @@
     shared = lax.all_to_all(shared, AXIS, 0, 0, tiled=True)
     two = jnp.concatenate([block, swapped(block, 1)], axis=0)
     own = jnp.concatenate([two, swapped(two, 2)], axis=0)
+    own, m2l = lax.optimization_barrier((own, operators(m2l_ops)))
     is_upper = me // 4 % 2 == 1
     low_side, high_side = own[:, :128], own[:, 128:]
     sibling = swapped(jnp.where(is_upper, low_side, high_side), 6)
@@ -475,7 +502,7 @@
     below = jnp.concatenate([below[64:], below[:64]], axis=0)
     above = jnp.concatenate([above[64:], above[:64]], axis=0)
     table = jnp.asarray(device_level_table())
-    partial, device_ops = far_field(table, own, below, above, operators(m2l_ops))
+    partial, device_ops, root_ops = far_field(table, own, below, above, m2l, root_ops)
     return top_levels(table, partial, device_ops, shared, root_ops)
 
 

time: 51.4 us -> 52.3 us (1.018)
  Pallas kernels: 18.1 us -> 22.2 us
  waiting for transfers between devices: 10 us -> 7.3 us
    pallas_call x1, Pallas kernels: 3.36 us -> 6.25 us  [far_field(): pl.pallas_call(far_kernel, out_shape=(jax.ShapeDtypeStruct((80, RANK), F3...]
    ppermute x3, waiting for transfers between devices: 3.6 us -> 0.84 us  [swapped(): return lax.ppermute(value, AXIS, [(s, s ^ mask) for s in range(devices)])]
    all_to_all x1, starting transfers between devices: 14.6 us -> 13.1 us  [body(): shared = lax.all_to_all(shared, AXIS, 0, 0, tiled=True)]
    pallas_call x1, Pallas kernels: 2.85 us -> 4.39 us  [operators(): pl.pallas_call(operators_kernel, out_shape=pltpu.HBM(m2l_ops.shape, BF16)...]
    ppermute x3, starting transfers between devices: 6.96 us -> 8.16 us  [swapped(): return lax.ppermute(value, AXIS, [(s, s ^ mask) for s in range(devices)])]
  transfers between devices with their start and end apart: 5 -> 5, of which waited for: 3 -> 2; matrix products, arithmetic and copies ran while one was open for 0% -> 0% of each run, Pallas kernels for 12% -> 20%
where the time goes in v4:
time: 52.3 us; the launch traced here: 52.2 us
  Pallas kernels  22.2 us (42%)
  starting transfers between devices  21.9 us (42%)
  waiting for transfers between devices  7.3 us (14%)
  between operations  0.77 us (1%)
    all_to_all x1, starting transfers between devices, body(): shared = lax.all_to_all(shared, AXIS, 0, 0, tiled=True)  13.1 us
    pallas_call x1, Pallas kernels, upward(): pl.pallas_call(upward_kernel, out_shape=(pltpu.VMEM((devices, 128), F32),...  9.74 us
    ppermute x3, starting transfers between devices, swapped(): return lax.ppermute(value, AXIS, [(s, s ^ mask) for s in range(devices)])  8.16 us
    all_to_all x1, waiting for transfers between devices, body(): shared = lax.all_to_all(shared, AXIS, 0, 0, tiled=True)  6.46 us
    pallas_call x1, Pallas kernels, far_field(): pl.pallas_call(far_kernel, out_shape=(jax.ShapeDtypeStruct((80, RANK), F3...  6.25 us
    pallas_call x1, Pallas kernels, operators(): pl.pallas_call(operators_kernel, out_shape=pltpu.HBM(m2l_ops.shape, BF16)...  4.39 us
    pallas_call x1, Pallas kernels, top_levels(): pl.pallas_call(top_kernel, out_shape=(jax.ShapeDtypeStruct((RANK, BOX_DEV...  1.8 us
  transfers between devices with their start and end apart: 5, of which 2 were waited for; matrix products, arithmetic and copies ran while one was open for 0% of the time, Pallas kernels for 20%

profile of v4, /device:TPU:1, one launch (start us, length us, event | category | flops | bytes accessed | tf_op | source)
XLA Modules:
  0.0 52.2 jit_solution(15621605973317945813)
XLA Ops:
  0.6 0.0 copy-start
  0.6 9.7 %upward.1 = (f32[256,128]{1,0:T(8,128)}, bf16[32,256]{1,0:T(8,128)(2,1)S(1)}) custom-call(f32[3,8192]{1,0:T(4,128)} %offsets_hbm.1, f32[3,8192]{1,0:T(4,128)} %forces_hbm.1, s32[64]{0:T(128)} %counts_hbm.1, f32[3,152,128]{2,1,0:T(8,128)} %constant.41.clone.surface_hbm, f32[8,152]{1,0:T(8,128)} %constant.42.clone.points_hbm, ...), custom_call_target="tpu_custom_call" | custom-call | tf_op jit(solution)/shard_map/upward/pallas_call | solution.py:389
  10.4 0.0 copy-start.1
  10.4 3.3 %collective-permute-start = (bf16[32,256]{1,0:T(8,128)(2,1)S(1)}, bf16[32,256]{1,0:T(8,128)(2,1)S(1)}, u32[]{:S(2)}, u32[]{:S(2)}) collective-permute-start(bf16[32,256]{1,0:T(8,128)(2,1)S(1)} %get-tuple-element.11), channel_id=1, source_target_pairs={{0,1},{1,0},{2,3},{3,2},{4,5},{5,4},{6,7},{7,6},{8,9},{9,8},{10,11... | collective-permute-start | bytes 49160 | tf_op jit(solution)/shard_map/ppermute | solution.py:475
  13.7 0.8 %collective-permute-done = bf16[32,256]{1,0:T(8,128)(2,1)S(1)} collective-permute-done((bf16[32,256]{1,0:T(8,128)(2,1)S(1)}, bf16[32,256]{1,0:T(8,128)(2,1)S(1)}, u32[]{:S(2)}, u32[]{:S(2)}) %collective-permute-start) | collective-permute-done | bytes 16416 | tf_op jit(solution)/shard_map/ppermute | solution.py:475
  14.6 0.0 collective-permute-start.1
  14.6 0.0 copy-done
  14.6 4.4 %operators.1.m2l_hbm = bf16[316,64,64]{2,1,0:T(8,128)(2,1)} custom-call(bf16[64,64,316]{2,1,0:T(8,128)(2,1)S(1)} %bitcast.7), custom_call_target="tpu_custom_call" | custom-call | tf_op jit(solution)/shard_map/operators/pallas_call | solution.py:411
  19.0 0.0 collective-permute-done.1
  19.0 0.7 %collective-permute-start.3 = (bf16[128,128]{1,0:T(8,128)(2,1)S(1)}, bf16[128,128]{1,0:T(8,128)(2,1)S(1)}, u32[]{:S(2)}, u32[]{:S(2)}) collective-permute-start(bf16[128,128]{1,0:T(8,128)(2,1)S(1)} %get-tuple-element.22), channel_id=1, source_target_pairs={{4,10},{5,11},{6,8},{7,9},{8,6},{9,7},{10,4},{11,5},{12,18},{13,19... | collective-permute-start | bytes 98312 | tf_op jit(solution)/shard_map/ppermute | solution.py:486
  19.7 4.8 %collective-permute-start.2 = (bf16[128,128]{1,0:T(8,128)(2,1)S(1)}, bf16[128,128]{1,0:T(8,128)(2,1)S(1)}, u32[]{:S(2)}, u32[]{:S(2)}) collective-permute-start(bf16[128,128]{1,0:T(8,128)(2,1)S(1)} %get-tuple-element.23), channel_id=1, source_target_pairs={{0,6},{1,7},{2,4},{3,5},{4,2},{5,3},{6,0},{7,1},{8,14},{9,15},{10,... | collective-permute-start | bytes 98312 | tf_op jit(solution)/shard_map/ppermute | solution.py:475
  24.5 13.1 %all-to-all-start = ((f32[256,1,128]{2,1,0:T(1,128)}), f32[256,1,128]{2,1,0:T(1,128)S(1)}, u32[]{:S(2)}, u32[]{:S(2)}) async-start(f32[256,1,128]{2,1,0:T(1,128)} %bitcast.3), calls=%async_computation | async-start | bytes 262144 | tf_op jit(solution)/shard_map/all_to_all | solution.py:492
  37.6 0.0 collective-permute-done.3
  37.6 0.0 collective-permute-done.2
  37.7 0.0 copy-done.1
  37.7 6.2 %far_field.1 = (f32[80,64]{1,0:T(8,128)S(1)}, bf16[12,64,64]{2,1,0:T(8,128)(2,1)S(1)}, bf16[63,64,64]{2,1,0:T(8,128)(2,1)S(1)}) custom-call(s32[8,24]{1,0:T(8,128)S(1)} %copy-done.1, bf16[128,256]{1,0:T(8,128)(2,1)S(1)} %pad_maximum_fusion.own, bf16[128,128]{1,0:T(8,128)(2,1)S(1)} %pad_maximum_fusion.2.below, bf16[128,128]{1,0:T(8,128)(2,1)S(1)} %pad_maximum_fusion.3.above, ...), custom_call_target="tpu_custom_call" | custom-call | tf_op jit(solution)/shard_map/far_field/pallas_call | solution.py:431
  43.9 6.5 %all-to-all-done = f32[256,1,128]{2,1,0:T(1,128)S(1)} async-done(((f32[256,1,128]{2,1,0:T(1,128)}), f32[256,1,128]{2,1,0:T(1,128)S(1)}, u32[]{:S(2)}, u32[]{:S(2)}) %all-to-all-start) | async-done | bytes 131104 | tf_op jit(solution)/shard_map/all_to_all | solution.py:492
  50.4 1.8 %top_levels.1 = (f32[64,73]{1,0:T(8,128)}, f32[32,64]{1,0:T(8,128)}) custom-call(s32[8,24]{1,0:T(8,128)S(1)} %copy-done.1, f32[80,64]{1,0:T(8,128)S(1)} %get-tuple-element.14.partial, bf16[12,64,64]{2,1,0:T(8,128)(2,1)S(1)} %get-tuple-element.15.device_ops, f32[256,128]{1,0:T(8,128)S(1)} %bitcast.8, bf16[63,64,64]{2,1,0:T(8,128)(2,1)S(1)} %get-tuple-element.17.root_ops), custom_call_target="tpu_custom_call" | custom-call | tf_op jit(solution)/shard_map/top_levels/pallas_call | solution.py:454
  (7 shorter events, 0.0 us)
Async XLA Ops:
  0.6 13.9 %copy-start = (bf16[316,64,64]{0,2,1:T(8,128)(2,1)S(1)}, bf16[316,64,64]{0,2,1:T(8,128)(2,1)}, u32[]{:S(2)}) copy-start(bf16[316,64,64]{0,2,1:T(8,128)(2,1)} %param.19) | copy-start | bytes 7766020
  10.4 27.3 %copy-start.1 = (s32[8,24]{1,0:T(8,128)S(1)}, s32[8,24]{1,0:T(8,128)}, u32[]{:S(2)}) copy-start(s32[8,24]{1,0:T(8,128)} %constant.44.clone.table) | copy-start | bytes 2308
  10.4 4.2 %collective-permute-start = (bf16[32,256]{1,0:T(8,128)(2,1)S(1)}, bf16[32,256]{1,0:T(8,128)(2,1)S(1)}, u32[]{:S(2)}, u32[]{:S(2)}) collective-permute-start(bf16[32,256]{1,0:T(8,128)(2,1)S(1)} %get-tuple-element.11), channel_id=1, source_target_pairs={{0,1},{1,0},{2,3},{3,2},{4,5},{5,4},{6,7},{7,6},{8,9},{9,8},{10,11... | collective-permute-start | bytes 49160 | tf_op jit(solution)/shard_map/ppermute | solution.py:475
  14.6 4.4 %collective-permute-start.1 = (bf16[64,256]{1,0:T(8,128)(2,1)S(1)}, bf16[64,256]{1,0:T(8,128)(2,1)S(1)}, u32[]{:S(2)}, u32[]{:S(2)}) collective-permute-start(bf16[64,256]{1,0:T(8,128)(2,1)S(1)} %pad_maximum_fusion.1), channel_id=1, source_target_pairs={{0,2},{1,3},{2,0},{3,1},{4,6},{5,7},{6,4},{7,5},{8,10},{9,11},{10,... | collective-permute-start | bytes 98312 | tf_op jit(solution)/shard_map/ppermute | solution.py:475
  19.0 18.6 %collective-permute-start.3 = (bf16[128,128]{1,0:T(8,128)(2,1)S(1)}, bf16[128,128]{1,0:T(8,128)(2,1)S(1)}, u32[]{:S(2)}, u32[]{:S(2)}) collective-permute-start(bf16[128,128]{1,0:T(8,128)(2,1)S(1)} %get-tuple-element.22), channel_id=1, source_target_pairs={{4,10},{5,11},{6,8},{7,9},{8,6},{9,7},{10,4},{11,5},{12,18},{13,19... | collective-permute-start | bytes 98312 | tf_op jit(solution)/shard_map/ppermute | solution.py:486
  19.7 17.9 %collective-permute-start.2 = (bf16[128,128]{1,0:T(8,128)(2,1)S(1)}, bf16[128,128]{1,0:T(8,128)(2,1)S(1)}, u32[]{:S(2)}, u32[]{:S(2)}) collective-permute-start(bf16[128,128]{1,0:T(8,128)(2,1)S(1)} %get-tuple-element.23), channel_id=1, source_target_pairs={{0,6},{1,7},{2,4},{3,5},{4,2},{5,3},{6,0},{7,1},{8,14},{9,15},{10,... | collective-permute-start | bytes 98312 | tf_op jit(solution)/shard_map/ppermute | solution.py:475
  24.5 25.9 %all-to-all-start = ((f32[256,1,128]{2,1,0:T(1,128)}), f32[256,1,128]{2,1,0:T(1,128)S(1)}, u32[]{:S(2)}, u32[]{:S(2)}) async-start(f32[256,1,128]{2,1,0:T(1,128)} %bitcast.3), calls=%async_computation | async-start | bytes 262144 | tf_op jit(solution)/shard_map/all_to_all | solution.py:492

commit v5 on v4

--- a/solution.py
+++ b/solution.py
@@ -231,18 +231,22 @@
         moved = dot_nt(unit, four)
         for half in range(2):
             turned[half, g * pitch : g * pitch + rows, :] = moved[:, half * 128 : half * 128 + 128]
-    part_size, all_leaving = (directions + 3) // 4, []
-    for d in range(directions):
+    lower = lax.broadcasted_iota(jnp.int32, (1, 128), 1) < RANK
+    count = directions // 2
+    part_size, all_leaving = (count + 3) // 4, []
+    for d in range(count):
         parts = []
         for half in range(2):
-            pair = turned[half, pl.ds(d, 16, stride=pitch), :]
-            parts += [pair, pltpu.roll(pair, RANK, 1)]
-        out[d] = jnp.concatenate(parts, axis=0)[:, :RANK].astype(BF16)
-        if (d + 1) % part_size == 0 or d + 1 == directions:
+            first = turned[half, pl.ds(d, 16, stride=pitch), :]
+            second = turned[half, pl.ds(d + count, 16, stride=pitch), :]
+            parts.append(jnp.where(lower, first, pltpu.roll(second, RANK, 1)))
+            parts.append(jnp.where(lower, pltpu.roll(first, RANK, 1), second))
+        out[d] = jnp.concatenate(parts, axis=0).astype(BF16)
+        if (d + 1) % part_size == 0 or d + 1 == count:
             chunk = d // part_size
-            first = chunk * part_size
+            start = chunk * part_size
             leaving = pltpu.make_async_copy(
-                out.at[first : d + 1], out_hbm.at[first : d + 1], out_sems.at[chunk]
+                out.at[start : d + 1], out_hbm.at[start : d + 1], out_sems.at[chunk]
             )
             leaving.start()
             all_leaving.append(leaving)
@@ -294,8 +298,18 @@
     first_rows = lax.broadcasted_iota(jnp.int32, (16, 128), 0) < 4
     total = jnp.zeros((80, RANK), F32)
     fetch_m2l.wait()
+    half_count = m2l.shape[0]
     for n in range(12):
-        device_ops[n] = m2l[table[me % 8, n]]
+        entry = table[me % 8, n]
+        beside = entry >= half_count
+        both = m2l[entry - jnp.where(beside, half_count, 0)].astype(F32)
+        both = jnp.where(beside, pltpu.roll(both, RANK, 1), both)
+        device_ops[n] = both[:, :RANK].astype(BF16)
+
+    def operator_of(entry):
+        lane = entry // half_count * RANK
+        return m2l[entry % half_count, :, lane : lane + RANK]
+
     for pair in range(49):
         v, w = pair // 7 - 3, pair % 7 - 3
         close = max(abs(v), abs(w)) < 2
@@ -311,7 +325,7 @@
         ]
         rows.append(jnp.concatenate(both, axis=1))
         left = jnp.concatenate(rows, axis=0)
-        operator = [m2l[DIRS[(u, v, w)]] for u in shifts]
+        operator = [operator_of(DIRS[(u, v, w)]) for u in shifts]
         if not close:
             left = left[:, : 7 * RANK]
         total = total + dot(left, jnp.concatenate(operator, axis=0))
@@ -410,13 +424,13 @@
     count = m2l_ops.shape[0]
     return pl.pallas_call(
         operators_kernel,
-        out_shape=pltpu.HBM(m2l_ops.shape, BF16),
+        out_shape=pltpu.HBM((count // 2, RANK, 2 * RANK), BF16),
         in_specs=[whole(pltpu.HBM)],
         out_specs=whole(pltpu.HBM),
         scratch_shapes=[
             pltpu.VMEM((RANK, RANK, count), BF16),
             pltpu.VMEM((2, 16 * (count + 5), 128), F32),
-            pltpu.VMEM(m2l_ops.shape, BF16),
+            pltpu.VMEM((count // 2, RANK, 2 * RANK), BF16),
             pltpu.SemaphoreType.DMA,
             pltpu.SemaphoreType.DMA((4,)),
         ],

time: 52.3 us -> 52 us (level)
  Pallas kernels: 22.2 us -> 21.2 us
  waiting for transfers between devices: 7.3 us -> 7.96 us
    pallas_call x1, Pallas kernels: 6.25 us -> 5.57 us  [far_field(): pl.pallas_call(far_kernel, out_shape=(jax.ShapeDtypeStruct((80, RANK), F3...]
    all_to_all x1, waiting for transfers between devices: 6.46 us -> 7.12 us  [body(): shared = lax.all_to_all(shared, AXIS, 0, 0, tiled=True)]
  transfers between devices with their start and end apart: 5 -> 5, of which waited for: 2 -> 2; matrix products, arithmetic and copies ran while one was open for 0% -> 0% of each run, Pallas kernels for 20% -> 19%
where the time goes in v5:
time: 52 us; the launch traced here: 51.9 us
  starting transfers between devices  21.9 us (42%)
  Pallas kernels  21.2 us (41%)
  waiting for transfers between devices  7.96 us (15%)
  between operations  0.77 us (1%)
    all_to_all x1, starting transfers between devices, body(): shared = lax.all_to_all(shared, AXIS, 0, 0, tiled=True)  13.1 us
    pallas_call x1, Pallas kernels, upward(): pl.pallas_call(upward_kernel, out_shape=(pltpu.VMEM((devices, 128), F32),...  9.75 us
    ppermute x3, starting transfers between devices, swapped(): return lax.ppermute(value, AXIS, [(s, s ^ mask) for s in range(devices)])  8.15 us
    all_to_all x1, waiting for transfers between devices, body(): shared = lax.all_to_all(shared, AXIS, 0, 0, tiled=True)  7.12 us
    pallas_call x1, Pallas kernels, far_field(): pl.pallas_call(far_kernel, out_shape=(jax.ShapeDtypeStruct((80, RANK), F3...  5.57 us
    pallas_call x1, Pallas kernels, operators(): pl.pallas_call(operators_kernel, out_shape=pltpu.HBM((count // 2, RANK, 2...  4.11 us
    pallas_call x1, Pallas kernels, top_levels(): pl.pallas_call(top_kernel, out_shape=(jax.ShapeDtypeStruct((RANK, BOX_DEV...  1.8 us
  transfers between devices with their start and end apart: 5, of which 2 were waited for; matrix products, arithmetic and copies ran while one was open for 0% of the time, Pallas kernels for 19%

profile of v5, /device:TPU:1, one launch (start us, length us, event | category | flops | bytes accessed | tf_op | source)
XLA Modules:
  0.0 51.9 jit_solution(16382327641439675929)
XLA Ops:
  0.6 0.0 copy-start
  0.6 9.7 %upward.1 = (f32[256,128]{1,0:T(8,128)}, bf16[32,256]{1,0:T(8,128)(2,1)S(1)}) custom-call(f32[3,8192]{1,0:T(4,128)} %offsets_hbm.1, f32[3,8192]{1,0:T(4,128)} %forces_hbm.1, s32[64]{0:T(128)} %counts_hbm.1, f32[3,152,128]{2,1,0:T(8,128)} %constant.41.clone.surface_hbm, f32[8,152]{1,0:T(8,128)} %constant.42.clone.points_hbm, ...), custom_call_target="tpu_custom_call" | custom-call | tf_op jit(solution)/shard_map/upward/pallas_call | solution.py:403
  10.4 3.3 %collective-permute-start = (bf16[32,256]{1,0:T(8,128)(2,1)S(1)}, bf16[32,256]{1,0:T(8,128)(2,1)S(1)}, u32[]{:S(2)}, u32[]{:S(2)}) collective-permute-start(bf16[32,256]{1,0:T(8,128)(2,1)S(1)} %get-tuple-element.11), channel_id=1, source_target_pairs={{0,1},{1,0},{2,3},{3,2},{4,5},{5,4},{6,7},{7,6},{8,9},{9,8},{10,11... | collective-permute-start | bytes 49160 | tf_op jit(solution)/shard_map/ppermute | solution.py:489
  13.7 0.8 %collective-permute-done = bf16[32,256]{1,0:T(8,128)(2,1)S(1)} collective-permute-done((bf16[32,256]{1,0:T(8,128)(2,1)S(1)}, bf16[32,256]{1,0:T(8,128)(2,1)S(1)}, u32[]{:S(2)}, u32[]{:S(2)}) %collective-permute-start) | collective-permute-done | bytes 16416 | tf_op jit(solution)/shard_map/ppermute | solution.py:489
  14.6 0.0 collective-permute-start.1
  14.6 0.0 copy-done
  14.6 0.0 copy-start.1
  14.6 4.1 %operators.1.m2l_hbm = bf16[158,64,128]{2,1,0:T(8,128)(2,1)} custom-call(bf16[64,64,316]{2,1,0:T(8,128)(2,1)S(1)} %bitcast.7), custom_call_target="tpu_custom_call" | custom-call | tf_op jit(solution)/shard_map/operators/pallas_call | solution.py:425
  18.7 0.0 collective-permute-done.1
  18.7 0.7 %collective-permute-start.3 = (bf16[128,128]{1,0:T(8,128)(2,1)S(1)}, bf16[128,128]{1,0:T(8,128)(2,1)S(1)}, u32[]{:S(2)}, u32[]{:S(2)}) collective-permute-start(bf16[128,128]{1,0:T(8,128)(2,1)S(1)} %get-tuple-element.22), channel_id=1, source_target_pairs={{4,10},{5,11},{6,8},{7,9},{8,6},{9,7},{10,4},{11,5},{12,18},{13,19... | collective-permute-start | bytes 98312 | tf_op jit(solution)/shard_map/ppermute | solution.py:500
  19.4 4.8 %collective-permute-start.2 = (bf16[128,128]{1,0:T(8,128)(2,1)S(1)}, bf16[128,128]{1,0:T(8,128)(2,1)S(1)}, u32[]{:S(2)}, u32[]{:S(2)}) collective-permute-start(bf16[128,128]{1,0:T(8,128)(2,1)S(1)} %get-tuple-element.23), channel_id=1, source_target_pairs={{0,6},{1,7},{2,4},{3,5},{4,2},{5,3},{6,0},{7,1},{8,14},{9,15},{10,... | collective-permute-start | bytes 98312 | tf_op jit(solution)/shard_map/ppermute | solution.py:489
  24.2 13.1 %all-to-all-start = ((f32[256,1,128]{2,1,0:T(1,128)}), f32[256,1,128]{2,1,0:T(1,128)S(1)}, u32[]{:S(2)}, u32[]{:S(2)}) async-start(f32[256,1,128]{2,1,0:T(1,128)} %bitcast.3), calls=%async_computation | async-start | bytes 262144 | tf_op jit(solution)/shard_map/all_to_all | solution.py:506
  37.3 0.0 collective-permute-done.3
  37.3 0.0 collective-permute-done.2
  37.4 0.0 copy-done.1
  37.4 5.6 %far_field.1 = (f32[80,64]{1,0:T(8,128)S(1)}, bf16[12,64,64]{2,1,0:T(8,128)(2,1)S(1)}, bf16[63,64,64]{2,1,0:T(8,128)(2,1)S(1)}) custom-call(s32[8,24]{1,0:T(8,128)S(1)} %copy-done.1, bf16[128,256]{1,0:T(8,128)(2,1)S(1)} %pad_maximum_fusion.own, bf16[128,128]{1,0:T(8,128)(2,1)S(1)} %pad_maximum_fusion.2.below, bf16[128,128]{1,0:T(8,128)(2,1)S(1)} %pad_maximum_fusion.3.above, ...), custom_call_target="tpu_custom_call" | custom-call | tf_op jit(solution)/shard_map/far_field/pallas_call | solution.py:445
  43.0 7.1 %all-to-all-done = f32[256,1,128]{2,1,0:T(1,128)S(1)} async-done(((f32[256,1,128]{2,1,0:T(1,128)}), f32[256,1,128]{2,1,0:T(1,128)S(1)}, u32[]{:S(2)}, u32[]{:S(2)}) %all-to-all-start) | async-done | bytes 131104 | tf_op jit(solution)/shard_map/all_to_all | solution.py:506
  50.1 1.8 %top_levels.1 = (f32[64,73]{1,0:T(8,128)}, f32[32,64]{1,0:T(8,128)}) custom-call(s32[8,24]{1,0:T(8,128)S(1)} %copy-done.1, f32[80,64]{1,0:T(8,128)S(1)} %get-tuple-element.14.partial, bf16[12,64,64]{2,1,0:T(8,128)(2,1)S(1)} %get-tuple-element.15.device_ops, f32[256,128]{1,0:T(8,128)S(1)} %bitcast.8, bf16[63,64,64]{2,1,0:T(8,128)(2,1)S(1)} %get-tuple-element.17.root_ops), custom_call_target="tpu_custom_call" | custom-call | tf_op jit(solution)/shard_map/top_levels/pallas_call | solution.py:468
  (7 shorter events, 0.0 us)
Async XLA Ops:
  0.6 13.9 %copy-start = (bf16[316,64,64]{0,2,1:T(8,128)(2,1)S(1)}, bf16[316,64,64]{0,2,1:T(8,128)(2,1)}, u32[]{:S(2)}) copy-start(bf16[316,64,64]{0,2,1:T(8,128)(2,1)} %param.19) | copy-start | bytes 7766020
  10.4 4.2 %collective-permute-start = (bf16[32,256]{1,0:T(8,128)(2,1)S(1)}, bf16[32,256]{1,0:T(8,128)(2,1)S(1)}, u32[]{:S(2)}, u32[]{:S(2)}) collective-permute-start(bf16[32,256]{1,0:T(8,128)(2,1)S(1)} %get-tuple-element.11), channel_id=1, source_target_pairs={{0,1},{1,0},{2,3},{3,2},{4,5},{5,4},{6,7},{7,6},{8,9},{9,8},{10,11... | collective-permute-start | bytes 49160 | tf_op jit(solution)/shard_map/ppermute | solution.py:489
  14.6 4.1 %collective-permute-start.1 = (bf16[64,256]{1,0:T(8,128)(2,1)S(1)}, bf16[64,256]{1,0:T(8,128)(2,1)S(1)}, u32[]{:S(2)}, u32[]{:S(2)}) collective-permute-start(bf16[64,256]{1,0:T(8,128)(2,1)S(1)} %pad_maximum_fusion.1), channel_id=1, source_target_pairs={{0,2},{1,3},{2,0},{3,1},{4,6},{5,7},{6,4},{7,5},{8,10},{9,11},{10,... | collective-permute-start | bytes 98312 | tf_op jit(solution)/shard_map/ppermute | solution.py:489
  14.6 22.8 %copy-start.1 = (s32[8,24]{1,0:T(8,128)S(1)}, s32[8,24]{1,0:T(8,128)}, u32[]{:S(2)}) copy-start(s32[8,24]{1,0:T(8,128)} %constant.44.clone.table) | copy-start | bytes 2308
  18.7 18.6 %collective-permute-start.3 = (bf16[128,128]{1,0:T(8,128)(2,1)S(1)}, bf16[128,128]{1,0:T(8,128)(2,1)S(1)}, u32[]{:S(2)}, u32[]{:S(2)}) collective-permute-start(bf16[128,128]{1,0:T(8,128)(2,1)S(1)} %get-tuple-element.22), channel_id=1, source_target_pairs={{4,10},{5,11},{6,8},{7,9},{8,6},{9,7},{10,4},{11,5},{12,18},{13,19... | collective-permute-start | bytes 98312 | tf_op jit(solution)/shard_map/ppermute | solution.py:500
  19.4 17.9 %collective-permute-start.2 = (bf16[128,128]{1,0:T(8,128)(2,1)S(1)}, bf16[128,128]{1,0:T(8,128)(2,1)S(1)}, u32[]{:S(2)}, u32[]{:S(2)}) collective-permute-start(bf16[128,128]{1,0:T(8,128)(2,1)S(1)} %get-tuple-element.23), channel_id=1, source_target_pairs={{0,6},{1,7},{2,4},{3,5},{4,2},{5,3},{6,0},{7,1},{8,14},{9,15},{10,... | collective-permute-start | bytes 98312 | tf_op jit(solution)/shard_map/ppermute | solution.py:489
  24.2 25.9 %all-to-all-start = ((f32[256,1,128]{2,1,0:T(1,128)}), f32[256,1,128]{2,1,0:T(1,128)S(1)}, u32[]{:S(2)}, u32[]{:S(2)}) async-start(f32[256,1,128]{2,1,0:T(1,128)} %bitcast.3), calls=%async_computation | async-start | bytes 262144 | tf_op jit(solution)/shard_map/all_to_all | solution.py:506

commit v6 on v5

--- a/solution.py
+++ b/solution.py
@@ -216,7 +216,7 @@
     block[16:32, 128:256] = middle
 
 
-def operators_kernel(source_hbm, out_hbm, source, turned, out, sem, out_sems):
+def operators_kernel(source_hbm, out, source, turned, sem):
     fetch = pltpu.make_async_copy(source_hbm, source, sem)
     fetch.start()
     directions = source.shape[2]
@@ -233,7 +233,6 @@
             turned[half, g * pitch : g * pitch + rows, :] = moved[:, half * 128 : half * 128 + 128]
     lower = lax.broadcasted_iota(jnp.int32, (1, 128), 1) < RANK
     count = directions // 2
-    part_size, all_leaving = (count + 3) // 4, []
     for d in range(count):
         parts = []
         for half in range(2):
@@ -242,29 +241,14 @@
             parts.append(jnp.where(lower, first, pltpu.roll(second, RANK, 1)))
             parts.append(jnp.where(lower, pltpu.roll(first, RANK, 1), second))
         out[d] = jnp.concatenate(parts, axis=0).astype(BF16)
-        if (d + 1) % part_size == 0 or d + 1 == count:
-            chunk = d // part_size
-            start = chunk * part_size
-            leaving = pltpu.make_async_copy(
-                out.at[start : d + 1], out_hbm.at[start : d + 1], out_sems.at[chunk]
-            )
-            leaving.start()
-            all_leaving.append(leaving)
-    for leaving in all_leaving:
-        leaving.wait()
 
 
 def far_kernel(
-    table, own, below, above, picks_hbm, m2l_hbm, root_hbm, boxes, device_ops, root_ops,
-    picks, near, m2l, sem, m2l_sem, root_sem,
+    table, own, below, above, m2l, picks_hbm, boxes, device_ops, picks, near, sem
 ):
     me = lax.axis_index(AXIS)
     fetch = pltpu.make_async_copy(picks_hbm.at[me % 4], picks, sem)
     fetch.start()
-    fetch_m2l = pltpu.make_async_copy(m2l_hbm, m2l, m2l_sem)
-    fetch_m2l.start()
-    fetch_root = pltpu.make_async_copy(root_hbm, root_ops, root_sem)
-    fetch_root.start()
     lower = lax.broadcasted_iota(jnp.int32, (1, 128), 1) < RANK
 
     x01, x23, x45, x67 = below[...], own[:, 0:128], own[:, 128:256], above[...]
@@ -297,7 +281,6 @@
     level1_far = ((7, 3), (0, 10))
     first_rows = lax.broadcasted_iota(jnp.int32, (16, 128), 0) < 4
     total = jnp.zeros((80, RANK), F32)
-    fetch_m2l.wait()
     half_count = m2l.shape[0]
     for n in range(12):
         entry = table[me % 8, n]
@@ -329,7 +312,6 @@
         if not close:
             left = left[:, : 7 * RANK]
         total = total + dot(left, jnp.concatenate(operator, axis=0))
-    fetch_root.wait()
     boxes[...] = jnp.zeros(boxes.shape, F32)
     boxes[1:9, :] = total[64:72]
     for p in range(2):
@@ -339,7 +321,11 @@
             boxes[9 + 16 * x : 25 + 16 * x, :] = total[first : first + 16]
 
 
-def top_kernel(table, partial, device_ops, shared, root_ops, boxes, roots, base, shifted, turned):
+def top_kernel(
+    table, partial, device_ops, shared, root_hbm, boxes, roots, base, shifted, turned, root_ops, sem
+):
+    fetch = pltpu.make_async_copy(root_hbm, root_ops, sem)
+    fetch.start()
     me = lax.axis_index(AXIS)
     lower = lax.broadcasted_iota(jnp.int32, (1, 128), 1) < RANK
     gathered = shared[...]
@@ -350,21 +336,6 @@
     base[32:64, :] = jnp.where(lower, low_half, 0.0)
     shifted[31:63, :] = jnp.where(lower, 0.0, high_half)
     base[...] = base[...] + shifted[...]
-    total = jnp.zeros((NROOT, RANK), F32)
-    for distance in range(-31, 32, 2):
-        if distance == -1:
-            continue
-        source = base[32 + distance : 64 + distance, :]
-        first = distance + NROOT - 1
-        if distance == 1:
-            source = jnp.where(lower, 0.0, source)
-        if distance == 31:
-            total = total + dot(source[:, :RANK].astype(BF16), root_ops[first])
-            continue
-        operator = jnp.concatenate([root_ops[first], root_ops[first + 1]], axis=0)
-        total = total + dot(source.astype(BF16), operator)
-    roots[...] = total
-
     first_column = me // 8 * 2
     columns_total = lax.axis_size(AXIS) // 4
     far = jnp.zeros((8, RANK), F32)
@@ -381,6 +352,22 @@
     turned[0:80, 0:RANK] = partial[...]
     turned[0:1, 0:RANK] = far[0:1]
     boxes[...] = turned[...].T[:RANK, :BOX_DEV]
+
+    fetch.wait()
+    total = jnp.zeros((NROOT, RANK), F32)
+    for distance in range(-31, 32, 2):
+        if distance == -1:
+            continue
+        source = base[32 + distance : 64 + distance, :]
+        first = distance + NROOT - 1
+        if distance == 1:
+            source = jnp.where(lower, 0.0, source)
+        if distance == 31:
+            total = total + dot(source[:, :RANK].astype(BF16), root_ops[first])
+            continue
+        operator = jnp.concatenate([root_ops[first], root_ops[first + 1]], axis=0)
+        total = total + dot(source.astype(BF16), operator)
+    roots[...] = total
 
 
 def whole(space=pltpu.VMEM):
@@ -415,7 +402,7 @@
             pltpu.VMEM((LEAF_DEV, 4, NQ), F32),
             pltpu.SemaphoreType.DMA((len(operands),)),
         ],
-        compiler_params=pltpu.CompilerParams(vmem_limit_bytes=40 * 2**20),
+        compiler_params=pltpu.CompilerParams(vmem_limit_bytes=24 * 2**20),
         name="upward",
     )(*operands)
 
@@ -424,44 +411,38 @@
     count = m2l_ops.shape[0]
     return pl.pallas_call(
         operators_kernel,
-        out_shape=pltpu.HBM((count // 2, RANK, 2 * RANK), BF16),
+        out_shape=jax.ShapeDtypeStruct((count // 2, RANK, 2 * RANK), BF16),
         in_specs=[whole(pltpu.HBM)],
-        out_specs=whole(pltpu.HBM),
+        out_specs=whole(),
         scratch_shapes=[
             pltpu.VMEM((RANK, RANK, count), BF16),
             pltpu.VMEM((2, 16 * (count + 5), 128), F32),
-            pltpu.VMEM((count // 2, RANK, 2 * RANK), BF16),
             pltpu.SemaphoreType.DMA,
-            pltpu.SemaphoreType.DMA((4,)),
         ],
-        compiler_params=pltpu.CompilerParams(vmem_limit_bytes=28 * 2**20),
+        compiler_params=pltpu.CompilerParams(vmem_limit_bytes=16 * 2**20),
         name="operators",
-    )(jnp.transpose(m2l_ops, (1, 2, 0)))
-
-
-def far_field(table, own, below, above, m2l, root_ops):
-    held = (jnp.asarray(cross_section_picks()), m2l, root_ops)
+    )(pltpu.with_memory_space_constraint(jnp.transpose(m2l_ops, (1, 2, 0)), pltpu.HBM))
+
+
+def far_field(table, own, below, above, m2l):
+    held = (jnp.asarray(cross_section_picks()),)
     held = [pltpu.with_memory_space_constraint(x, pltpu.HBM) for x in held]
     return pl.pallas_call(
         far_kernel,
         out_shape=(
             jax.ShapeDtypeStruct((80, RANK), F32),
             jax.ShapeDtypeStruct((12, RANK, RANK), BF16),
-            jax.ShapeDtypeStruct(root_ops.shape, BF16),
         ),
-        in_specs=[whole(pltpu.SMEM), whole(), whole(), whole()] + [whole(pltpu.HBM)] * 3,
-        out_specs=(whole(),) * 3,
+        in_specs=[whole(pltpu.SMEM), whole(), whole(), whole(), whole()] + [whole(pltpu.HBM)],
+        out_specs=(whole(),) * 2,
         scratch_shapes=[
             pltpu.VMEM((49 * 32, 128), BF16),
             pltpu.VMEM((49 * 32, 11 * 128), BF16),
-            pltpu.VMEM(m2l.shape, BF16),
-            pltpu.SemaphoreType.DMA,
-            pltpu.SemaphoreType.DMA,
             pltpu.SemaphoreType.DMA,
         ],
-        compiler_params=pltpu.CompilerParams(vmem_limit_bytes=28 * 2**20),
+        compiler_params=pltpu.CompilerParams(vmem_limit_bytes=16 * 2**20),
         name="far_field",
-    )(table, own, below, above, *held)
+    )(table, own, below, above, m2l, *held)
 
 
 def top_levels(table, partial, device_ops, shared, root_ops):
@@ -471,16 +452,18 @@
             jax.ShapeDtypeStruct((RANK, BOX_DEV), F32),
             jax.ShapeDtypeStruct((NROOT, RANK), F32),
         ),
-        in_specs=[whole(pltpu.SMEM)] + [whole()] * 4,
+        in_specs=[whole(pltpu.SMEM)] + [whole()] * 3 + [whole(pltpu.HBM)],
         out_specs=(whole(), whole()),
         scratch_shapes=[
             pltpu.VMEM((96, 128), F32),
             pltpu.VMEM((96, 128), F32),
             pltpu.VMEM((128, 128), F32),
+            pltpu.VMEM(root_ops.shape, BF16),
+            pltpu.SemaphoreType.DMA,
         ],
         compiler_params=pltpu.CompilerParams(vmem_limit_bytes=16 * 2**20),
         name="top_levels",
-    )(table, partial, device_ops, shared, root_ops)
+    )(table, partial, device_ops, shared, pltpu.with_memory_space_constraint(root_ops, pltpu.HBM))
     return boxes.T, roots
 
 
@@ -516,7 +499,7 @@
     below = jnp.concatenate([below[64:], below[:64]], axis=0)
     above = jnp.concatenate([above[64:], above[:64]], axis=0)
     table = jnp.asarray(device_level_table())
-    partial, device_ops, root_ops = far_field(table, own, below, above, m2l, root_ops)
+    partial, device_ops = far_field(table, own, below, above, m2l)
     return top_levels(table, partial, device_ops, shared, root_ops)
 
 

time: 52 us -> 53.4 us (1.027)
  waiting for transfers between devices: 7.96 us -> 9.59 us
    all_to_all x1, waiting for transfers between devices: 7.12 us -> 8.74 us  [body(): shared = lax.all_to_all(shared, AXIS, 0, 0, tiled=True)]
    pallas_call x1, Pallas kernels: 5.57 us -> 3.97 us  [far_field(): pl.pallas_call(far_kernel, out_shape=(jax.ShapeDtypeStruct((80, RANK), F3...]
    pallas_call x1, Pallas kernels: 1.8 us -> 2.99 us  [top_levels(): pl.pallas_call(top_kernel, out_shape=(jax.ShapeDtypeStruct((RANK, BOX_DEV...]
  transfers between devices with their start and end apart: 5 -> 5, of which waited for: 2 -> 2; matrix products, arithmetic and copies ran while one was open for 0% -> 0% of each run, Pallas kernels for 19% -> 15%
where the time goes in v6:
time: 53.4 us; the launch traced here: 53.1 us
  starting transfers between devices  21.9 us (41%)
  Pallas kernels  20.7 us (39%)
  waiting for transfers between devices  9.59 us (18%)
  between operations  0.92 us (2%)
    all_to_all x1, starting transfers between devices, body(): shared = lax.all_to_all(shared, AXIS, 0, 0, tiled=True)  13.1 us
    pallas_call x1, Pallas kernels, upward(): pl.pallas_call(upward_kernel, out_shape=(pltpu.VMEM((devices, 128), F32),...  9.59 us
    all_to_all x1, waiting for transfers between devices, body(): shared = lax.all_to_all(shared, AXIS, 0, 0, tiled=True)  8.74 us
    ppermute x3, starting transfers between devices, swapped(): return lax.ppermute(value, AXIS, [(s, s ^ mask) for s in range(devices)])  8.16 us
    pallas_call x1, Pallas kernels, operators(): pl.pallas_call(operators_kernel, out_shape=jax.ShapeDtypeStruct((count //...  4.16 us
    pallas_call x1, Pallas kernels, far_field(): pl.pallas_call(far_kernel, out_shape=(jax.ShapeDtypeStruct((80, RANK), F3...  3.97 us
    pallas_call x1, Pallas kernels, top_levels(): pl.pallas_call(top_kernel, out_shape=(jax.ShapeDtypeStruct((RANK, BOX_DEV...  2.99 us
  transfers between devices with their start and end apart: 5, of which 2 were waited for; matrix products, arithmetic and copies ran while one was open for 0% of the time, Pallas kernels for 15%

profile of v6, /device:TPU:1, one launch (start us, length us, event | category | flops | bytes accessed | tf_op | source)
XLA Modules:
  0.0 53.1 jit_solution(7893378948447024180)
XLA Ops:
  0.6 9.6 %upward.1 = (f32[256,128]{1,0:T(8,128)}, bf16[32,256]{1,0:T(8,128)(2,1)S(1)}) custom-call(f32[3,8192]{1,0:T(4,128)} %offsets_hbm.1, f32[3,8192]{1,0:T(4,128)} %forces_hbm.1, s32[64]{0:T(128)} %counts_hbm.1, f32[3,152,128]{2,1,0:T(8,128)} %constant.41.clone.surface_hbm, f32[8,152]{1,0:T(8,128)} %constant.42.clone.points_hbm, ...), custom_call_target="tpu_custom_call" | custom-call | tf_op jit(solution)/shard_map/upward/pallas_call | solution.py:390
  10.2 3.3 %collective-permute-start = (bf16[32,256]{1,0:T(8,128)(2,1)S(1)}, bf16[32,256]{1,0:T(8,128)(2,1)S(1)}, u32[]{:S(2)}, u32[]{:S(2)}) collective-permute-start(bf16[32,256]{1,0:T(8,128)(2,1)S(1)} %get-tuple-element.10), channel_id=1, source_target_pairs={{0,1},{1,0},{2,3},{3,2},{4,5},{5,4},{6,7},{7,6},{8,9},{9,8},{10,11... | collective-permute-start | bytes 49160 | tf_op jit(solution)/shard_map/ppermute | solution.py:472
  13.6 0.8 %collective-permute-done = bf16[32,256]{1,0:T(8,128)(2,1)S(1)} collective-permute-done((bf16[32,256]{1,0:T(8,128)(2,1)S(1)}, bf16[32,256]{1,0:T(8,128)(2,1)S(1)}, u32[]{:S(2)}, u32[]{:S(2)}) %collective-permute-start) | collective-permute-done | bytes 16416 | tf_op jit(solution)/shard_map/ppermute | solution.py:472
  14.4 0.0 collective-permute-start.1
  14.4 0.0 copy-start
  14.4 4.2 %operators.1.m2l = bf16[158,64,128]{2,1,0:T(8,128)(2,1)S(1)} custom-call(bf16[64,64,316]{2,1,0:T(8,128)(2,1)} %bitcast.8), custom_call_target="tpu_custom_call" | custom-call | tf_op jit(solution)/shard_map/operators/pallas_call | solution.py:412
  18.6 0.0 collective-permute-done.1
  18.6 0.7 %collective-permute-start.3 = (bf16[128,128]{1,0:T(8,128)(2,1)S(1)}, bf16[128,128]{1,0:T(8,128)(2,1)S(1)}, u32[]{:S(2)}, u32[]{:S(2)}) collective-permute-start(bf16[128,128]{1,0:T(8,128)(2,1)S(1)} %get-tuple-element.20), channel_id=1, source_target_pairs={{4,10},{5,11},{6,8},{7,9},{8,6},{9,7},{10,4},{11,5},{12,18},{13,19... | collective-permute-start | bytes 98312 | tf_op jit(solution)/shard_map/ppermute | solution.py:483
  19.3 4.8 %collective-permute-start.2 = (bf16[128,128]{1,0:T(8,128)(2,1)S(1)}, bf16[128,128]{1,0:T(8,128)(2,1)S(1)}, u32[]{:S(2)}, u32[]{:S(2)}) collective-permute-start(bf16[128,128]{1,0:T(8,128)(2,1)S(1)} %get-tuple-element.21), channel_id=1, source_target_pairs={{0,6},{1,7},{2,4},{3,5},{4,2},{5,3},{6,0},{7,1},{8,14},{9,15},{10,... | collective-permute-start | bytes 98312 | tf_op jit(solution)/shard_map/ppermute | solution.py:472
  24.1 13.1 %all-to-all-start = ((f32[256,1,128]{2,1,0:T(1,128)}), f32[256,1,128]{2,1,0:T(1,128)S(1)}, u32[]{:S(2)}, u32[]{:S(2)}) async-start(f32[256,1,128]{2,1,0:T(1,128)} %bitcast.3), calls=%async_computation | async-start | bytes 262144 | tf_op jit(solution)/shard_map/all_to_all | solution.py:489
  37.2 0.0 collective-permute-done.3
  37.2 0.0 collective-permute-done.2
  37.3 0.0 copy-done
  37.3 4.0 %far_field.1 = (f32[80,64]{1,0:T(8,128)S(1)}, bf16[12,64,64]{2,1,0:T(8,128)(2,1)S(1)}) custom-call(s32[8,24]{1,0:T(8,128)S(1)} %copy-done, bf16[128,256]{1,0:T(8,128)(2,1)S(1)} %pad_maximum_fusion.own, bf16[128,128]{1,0:T(8,128)(2,1)S(1)} %pad_maximum_fusion.2.below, bf16[128,128]{1,0:T(8,128)(2,1)S(1)} %pad_maximum_fusion.3.above, ...), custom_call_target="tpu_custom_call" | custom-call | tf_op jit(solution)/shard_map/far_field/pallas_call | solution.py:430
  41.3 8.7 %all-to-all-done = f32[256,1,128]{2,1,0:T(1,128)S(1)} async-done(((f32[256,1,128]{2,1,0:T(1,128)}), f32[256,1,128]{2,1,0:T(1,128)S(1)}, u32[]{:S(2)}, u32[]{:S(2)}) %all-to-all-start) | async-done | bytes 131104 | tf_op jit(solution)/shard_map/all_to_all | solution.py:489
  50.0 3.0 %top_levels.1 = (f32[64,73]{1,0:T(8,128)}, f32[32,64]{1,0:T(8,128)}) custom-call(s32[8,24]{1,0:T(8,128)S(1)} %copy-done, f32[80,64]{1,0:T(8,128)S(1)} %get-tuple-element.13.partial, bf16[12,64,64]{2,1,0:T(8,128)(2,1)S(1)} %get-tuple-element.14.device_ops, f32[256,128]{1,0:T(8,128)S(1)} %bitcast.7, bf16[63,64,64]{2,1,0:T(8,128)(2,1)} %root_hbm.1), custom_call_target="tpu_custom_call" | custom-call | tf_op jit(solution)/shard_map/top_levels/pallas_call | solution.py:449
  (7 shorter events, 0.0 us)
Async XLA Ops:
  10.2 4.2 %collective-permute-start = (bf16[32,256]{1,0:T(8,128)(2,1)S(1)}, bf16[32,256]{1,0:T(8,128)(2,1)S(1)}, u32[]{:S(2)}, u32[]{:S(2)}) collective-permute-start(bf16[32,256]{1,0:T(8,128)(2,1)S(1)} %get-tuple-element.10), channel_id=1, source_target_pairs={{0,1},{1,0},{2,3},{3,2},{4,5},{5,4},{6,7},{7,6},{8,9},{9,8},{10,11... | collective-permute-start | bytes 49160 | tf_op jit(solution)/shard_map/ppermute | solution.py:472
  14.4 4.2 %collective-permute-start.1 = (bf16[64,256]{1,0:T(8,128)(2,1)S(1)}, bf16[64,256]{1,0:T(8,128)(2,1)S(1)}, u32[]{:S(2)}, u32[]{:S(2)}) collective-permute-start(bf16[64,256]{1,0:T(8,128)(2,1)S(1)} %pad_maximum_fusion.1), channel_id=1, source_target_pairs={{0,2},{1,3},{2,0},{3,1},{4,6},{5,7},{6,4},{7,5},{8,10},{9,11},{10,... | collective-permute-start | bytes 98312 | tf_op jit(solution)/shard_map/ppermute | solution.py:472
  14.4 22.9 %copy-start = (s32[8,24]{1,0:T(8,128)S(1)}, s32[8,24]{1,0:T(8,128)}, u32[]{:S(2)}) copy-start(s32[8,24]{1,0:T(8,128)} %constant.44.clone.table) | copy-start | bytes 2308
  18.6 18.6 %collective-permute-start.3 = (bf16[128,128]{1,0:T(8,128)(2,1)S(1)}, bf16[128,128]{1,0:T(8,128)(2,1)S(1)}, u32[]{:S(2)}, u32[]{:S(2)}) collective-permute-start(bf16[128,128]{1,0:T(8,128)(2,1)S(1)} %get-tuple-element.20), channel_id=1, source_target_pairs={{4,10},{5,11},{6,8},{7,9},{8,6},{9,7},{10,4},{11,5},{12,18},{13,19... | collective-permute-start | bytes 98312 | tf_op jit(solution)/shard_map/ppermute | solution.py:483
  19.3 17.9 %collective-permute-start.2 = (bf16[128,128]{1,0:T(8,128)(2,1)S(1)}, bf16[128,128]{1,0:T(8,128)(2,1)S(1)}, u32[]{:S(2)}, u32[]{:S(2)}) collective-permute-start(bf16[128,128]{1,0:T(8,128)(2,1)S(1)} %get-tuple-element.21), channel_id=1, source_target_pairs={{0,6},{1,7},{2,4},{3,5},{4,2},{5,3},{6,0},{7,1},{8,14},{9,15},{10,... | collective-permute-start | bytes 98312 | tf_op jit(solution)/shard_map/ppermute | solution.py:472
  24.1 25.9 %all-to-all-start = ((f32[256,1,128]{2,1,0:T(1,128)}), f32[256,1,128]{2,1,0:T(1,128)S(1)}, u32[]{:S(2)}, u32[]{:S(2)}) async-start(f32[256,1,128]{2,1,0:T(1,128)} %bitcast.3), calls=%async_computation | async-start | bytes 262144 | tf_op jit(solution)/shard_map/all_to_all | solution.py:489

commit v7 on v3

--- a/solution.py
+++ b/solution.py
@@ -19,7 +19,7 @@
 NROOT = 32
 AXIS = "morton"
 CHECK_RADIUS = 1.475
-LEAF_UNROLL = 16
+LEAF_UNROLL = 64
 
 F32 = jnp.float32
 BF16 = jnp.bfloat16
@@ -99,13 +99,13 @@
 
 
 def split(x):
+    high = x.astype(BF16)
+    return high, (x - high.astype(F32)).astype(BF16)
+
+
+def stacked(x):
     high = x.astype(BF16).astype(F32)
-    return high, x - high
-
-
-def stacked(x):
-    high, low = split(x)
-    return jnp.concatenate([high, low], axis=0).astype(BF16)
+    return jnp.concatenate([high, x - high], axis=0).astype(BF16)
 
 
 def dot(a, b):
@@ -159,8 +159,8 @@
             [jnp.concatenate([f, zero], axis=0), jnp.concatenate([-u, one], axis=0)], axis=1
         )
         left = stacked(left)
-        top = dot_nt(left, high.astype(BF16))
-        rest = dot_nt(left, low.astype(BF16))
+        top = dot_nt(left, high)
+        rest = dot_nt(left, low)
         sums = top[0:4] + (top[4:8] + rest[0:4])
         octant = (l >> 4 & 1) * 4 + (l >> 2 & 1) * 2 + (l & 1)
         parent = (l >> 5 & 1) * 4 + (l >> 3 & 1) * 2 + (l >> 1 & 1)
@@ -175,11 +175,10 @@
     for s in range(3):
         rows = check[:, s, :] + check[:, 3, :] * points[s : s + 1, :]
         w_high, w_low = split(uc2ue[s * NQ : (s + 1) * NQ, :])
-        density = density + product(rows, w_high.astype(BF16), w_low.astype(BF16))
+        density = density + product(rows, w_high, w_low)
     shrink = compress[...]
     shrink = jnp.concatenate([shrink, shrink], axis=0)
     s_high, s_low = split(shrink)
-    s_high, s_low = s_high.astype(BF16), s_low.astype(BF16)
     lower = lax.broadcasted_iota(jnp.int32, (1, 128), 1) < RANK
     leaves = product(density, s_high, s_low, dot_nt).astype(BF16)
     leaves = dot(order[...], leaves)
@@ -190,7 +189,6 @@
     parents = jnp.zeros((8, NCOEF), F32)
     for o in range(8):
         w_high, w_low = split(m2m[o])
-        w_high, w_low = w_high.astype(BF16), w_low.astype(BF16)
         m2m_high[o] = w_high
         m2m_low[o] = w_low
         parents = parents + product(density[o * 8 : o * 8 + 8], w_high, w_low)
@@ -198,7 +196,7 @@
     middle = jnp.where(lower, middle[0:4], middle[4:8])
 
     def one_row(x, w_high, w_low, dot=dot):
-        high, low = split(x)
+        high, low = (part.astype(F32) for part in split(x))
         row = lax.broadcasted_iota(jnp.int32, (8, 1), 0)
         both = jnp.where(row == 0, high, jnp.where(row == 1, low, 0.0)).astype(BF16)
         top = dot(both, w_high)

time: 51.4 us -> 51 us (level)
  no operation moved by 1% of the time
where the time goes in v7:
time: 51 us; the launch traced here: 50.9 us
  starting transfers between devices  22.2 us (44%)
  Pallas kernels  17.8 us (35%)
  waiting for transfers between devices  10 us (20%)
  between operations  0.78 us (2%)
    all_to_all x1, starting transfers between devices, body(): shared = lax.all_to_all(shared, AXIS, 0, 0, tiled=True)  14.6 us
    pallas_call x1, Pallas kernels, upward(): pl.pallas_call(upward_kernel, out_shape=(pltpu.VMEM((devices, 128), F32),...  9.75 us
    ppermute x3, starting transfers between devices, swapped(): return lax.ppermute(value, AXIS, [(s, s ^ mask) for s in range(devices)])  6.96 us
    all_to_all x1, waiting for transfers between devices, body(): shared = lax.all_to_all(shared, AXIS, 0, 0, tiled=True)  6.43 us
    ppermute x3, waiting for transfers between devices, swapped(): return lax.ppermute(value, AXIS, [(s, s ^ mask) for s in range(devices)])  3.6 us
    pallas_call x1, Pallas kernels, far_field(): pl.pallas_call(far_kernel, out_shape=(jax.ShapeDtypeStruct((80, RANK), F3...  3.36 us
    pallas_call x1, Pallas kernels, operators(): pl.pallas_call(operators_kernel, out_shape=jax.ShapeDtypeStruct(m2l_ops.s...  2.85 us
    pallas_call x1, Pallas kernels, top_levels(): pl.pallas_call(top_kernel, out_shape=(jax.ShapeDtypeStruct((RANK, BOX_DEV...  1.8 us
  transfers between devices with their start and end apart: 5, of which 3 were waited for; matrix products, arithmetic and copies ran while one was open for 0% of the time, Pallas kernels for 12%

profile of v7, /device:TPU:1, one launch (start us, length us, event | category | flops | bytes accessed | tf_op | source)
XLA Modules:
  0.0 50.9 jit_solution(5159481414290746535)
XLA Ops:
  0.6 0.0 copy-start
  0.6 9.8 %upward.1 = (f32[256,128]{1,0:T(8,128)}, bf16[32,256]{1,0:T(8,128)(2,1)S(1)}) custom-call(f32[3,8192]{1,0:T(4,128)} %offsets_hbm.1, f32[3,8192]{1,0:T(4,128)} %forces_hbm.1, s32[64]{0:T(128)} %counts_hbm.1, f32[3,152,128]{2,1,0:T(8,128)} %constant.41.clone.surface_hbm, f32[8,152]{1,0:T(8,128)} %constant.42.clone.points_hbm, ...), custom_call_target="tpu_custom_call" | custom-call | tf_op jit(solution)/shard_map/upward/pallas_call | solution.py:369
  10.4 0.0 copy-start.3
  10.4 3.3 %collective-permute-start = (bf16[32,256]{1,0:T(8,128)(2,1)S(1)}, bf16[32,256]{1,0:T(8,128)(2,1)S(1)}, u32[]{:S(2)}, u32[]{:S(2)}) collective-permute-start(bf16[32,256]{1,0:T(8,128)(2,1)S(1)} %get-tuple-element.8), channel_id=1, source_target_pairs={{0,1},{1,0},{2,3},{3,2},{4,5},{5,4},{6,7},{7,6},{8,9},{9,8},{10,11... | collective-permute-start | bytes 49160 | tf_op jit(solution)/shard_map/ppermute | solution.py:447
  13.7 0.8 %collective-permute-done = bf16[32,256]{1,0:T(8,128)(2,1)S(1)} collective-permute-done((bf16[32,256]{1,0:T(8,128)(2,1)S(1)}, bf16[32,256]{1,0:T(8,128)(2,1)S(1)}, u32[]{:S(2)}, u32[]{:S(2)}) %collective-permute-start) | collective-permute-done | bytes 16416 | tf_op jit(solution)/shard_map/ppermute | solution.py:447
  14.6 0.0 collective-permute-start.1
  14.6 2.8 %collective-permute-done.1 = bf16[64,256]{1,0:T(8,128)(2,1)S(1)} collective-permute-done((bf16[64,256]{1,0:T(8,128)(2,1)S(1)}, bf16[64,256]{1,0:T(8,128)(2,1)S(1)}, u32[]{:S(2)}, u32[]{:S(2)}) %collective-permute-start.1) | collective-permute-done | bytes 32800 | tf_op jit(solution)/shard_map/ppermute | solution.py:447
  17.4 0.7 %collective-permute-start.3 = (bf16[128,128]{1,0:T(8,128)(2,1)S(1)}, bf16[128,128]{1,0:T(8,128)(2,1)S(1)}, u32[]{:S(2)}, u32[]{:S(2)}) collective-permute-start(bf16[128,128]{1,0:T(8,128)(2,1)S(1)} %get-tuple-element.16), channel_id=1, source_target_pairs={{4,10},{5,11},{6,8},{7,9},{8,6},{9,7},{10,4},{11,5},{12,18},{13,19... | collective-permute-start | bytes 98312 | tf_op jit(solution)/shard_map/ppermute | solution.py:458
  18.0 3.6 %collective-permute-start.2 = (bf16[128,128]{1,0:T(8,128)(2,1)S(1)}, bf16[128,128]{1,0:T(8,128)(2,1)S(1)}, u32[]{:S(2)}, u32[]{:S(2)}) collective-permute-start(bf16[128,128]{1,0:T(8,128)(2,1)S(1)} %get-tuple-element.17), channel_id=1, source_target_pairs={{0,6},{1,7},{2,4},{3,5},{4,2},{5,3},{6,0},{7,1},{8,14},{9,15},{10,... | collective-permute-start | bytes 98312 | tf_op jit(solution)/shard_map/ppermute | solution.py:447
  21.7 14.6 %all-to-all-start = ((f32[256,1,128]{2,1,0:T(1,128)}), f32[256,1,128]{2,1,0:T(1,128)S(1)}, u32[]{:S(2)}, u32[]{:S(2)}) async-start(f32[256,1,128]{2,1,0:T(1,128)} %bitcast.3), calls=%async_computation | async-start | bytes 262144 | tf_op jit(solution)/shard_map/all_to_all | solution.py:464
  36.3 0.0 copy-start.1
  36.3 0.0 copy-done
  36.3 2.9 %operators.1.m2l = bf16[316,64,64]{2,1,0:T(8,128)(2,1)S(1)} custom-call(bf16[64,64,316]{2,1,0:T(8,128)(2,1)S(1)} %bitcast.7), custom_call_target="tpu_custom_call" | custom-call | tf_op jit(solution)/shard_map/operators/pallas_call | solution.py:391
  39.1 0.0 copy-start.2
  39.2 0.0 collective-permute-done.3
  39.2 0.0 collective-permute-done.2
  39.2 0.0 copy-done.3
  39.3 0.0 copy-done.1
  39.3 3.4 %far_field.1 = (f32[80,64]{1,0:T(8,128)S(1)}, bf16[12,64,64]{2,1,0:T(8,128)(2,1)S(1)}) custom-call(s32[8,24]{1,0:T(8,128)S(1)} %copy-done.3, bf16[128,256]{1,0:T(8,128)(2,1)S(1)} %constant_dynamic-update-slice_fusion.own, bf16[128,128]{1,0:T(8,128)(2,1)S(1)} %pad_maximum_fusion.1.below, bf16[128,128]{1,0:T(8,128)(2,1)S(1)} %pad_maximum_fusion.2.above, ...), custom_call_target="tpu_custom_call" | custom-call | tf_op jit(solution)/shard_map/far_field/pallas_call | solution.py:407
  42.6 6.4 %all-to-all-done = f32[256,1,128]{2,1,0:T(1,128)S(1)} async-done(((f32[256,1,128]{2,1,0:T(1,128)}), f32[256,1,128]{2,1,0:T(1,128)S(1)}, u32[]{:S(2)}, u32[]{:S(2)}) %all-to-all-start) | async-done | bytes 131104 | tf_op jit(solution)/shard_map/all_to_all | solution.py:464
  49.1 0.0 copy-done.2
  49.1 1.8 %top_levels.1 = (f32[64,73]{1,0:T(8,128)}, f32[32,64]{1,0:T(8,128)}) custom-call(s32[8,24]{1,0:T(8,128)S(1)} %copy-done.3, f32[80,64]{1,0:T(8,128)S(1)} %get-tuple-element.9.partial, bf16[12,64,64]{2,1,0:T(8,128)(2,1)S(1)} %get-tuple-element.10.device_ops, f32[256,128]{1,0:T(8,128)S(1)} %bitcast.8, bf16[63,64,64]{2,1,0:T(8,128)(2,1)S(1)} %copy-done.2), custom_call_target="tpu_custom_call" | custom-call | tf_op jit(solution)/shard_map/top_levels/pallas_call | solution.py:426
  (9 shorter events, 0.0 us)
Async XLA Ops:
  0.6 35.7 %copy-start = (bf16[316,64,64]{0,2,1:T(8,128)(2,1)S(1)}, bf16[316,64,64]{0,2,1:T(8,128)(2,1)}, u32[]{:S(2)}) copy-start(bf16[316,64,64]{0,2,1:T(8,128)(2,1)} %param.19) | copy-start | bytes 7766020
  10.4 28.8 %copy-start.3 = (s32[8,24]{1,0:T(8,128)S(1)}, s32[8,24]{1,0:T(8,128)}, u32[]{:S(2)}) copy-start(s32[8,24]{1,0:T(8,128)} %constant.44.clone.table) | copy-start | bytes 2308
  10.4 4.2 %collective-permute-start = (bf16[32,256]{1,0:T(8,128)(2,1)S(1)}, bf16[32,256]{1,0:T(8,128)(2,1)S(1)}, u32[]{:S(2)}, u32[]{:S(2)}) collective-permute-start(bf16[32,256]{1,0:T(8,128)(2,1)S(1)} %get-tuple-element.8), channel_id=1, source_target_pairs={{0,1},{1,0},{2,3},{3,2},{4,5},{5,4},{6,7},{7,6},{8,9},{9,8},{10,11... | collective-permute-start | bytes 49160 | tf_op jit(solution)/shard_map/ppermute | solution.py:447
  14.6 2.8 %collective-permute-start.1 = (bf16[64,256]{1,0:T(8,128)(2,1)S(1)}, bf16[64,256]{1,0:T(8,128)(2,1)S(1)}, u32[]{:S(2)}, u32[]{:S(2)}) collective-permute-start(bf16[64,256]{1,0:T(8,128)(2,1)S(1)} %pad_maximum_fusion), channel_id=1, source_target_pairs={{0,2},{1,3},{2,0},{3,1},{4,6},{5,7},{6,4},{7,5},{8,10},{9,11},{10,... | collective-permute-start | bytes 98312 | tf_op jit(solution)/shard_map/ppermute | solution.py:447
  17.4 21.8 %collective-permute-start.3 = (bf16[128,128]{1,0:T(8,128)(2,1)S(1)}, bf16[128,128]{1,0:T(8,128)(2,1)S(1)}, u32[]{:S(2)}, u32[]{:S(2)}) collective-permute-start(bf16[128,128]{1,0:T(8,128)(2,1)S(1)} %get-tuple-element.16), channel_id=1, source_target_pairs={{4,10},{5,11},{6,8},{7,9},{8,6},{9,7},{10,4},{11,5},{12,18},{13,19... | collective-permute-start | bytes 98312 | tf_op jit(solution)/shard_map/ppermute | solution.py:458
  18.0 21.1 %collective-permute-start.2 = (bf16[128,128]{1,0:T(8,128)(2,1)S(1)}, bf16[128,128]{1,0:T(8,128)(2,1)S(1)}, u32[]{:S(2)}, u32[]{:S(2)}) collective-permute-start(bf16[128,128]{1,0:T(8,128)(2,1)S(1)} %get-tuple-element.17), channel_id=1, source_target_pairs={{0,6},{1,7},{2,4},{3,5},{4,2},{5,3},{6,0},{7,1},{8,14},{9,15},{10,... | collective-permute-start | bytes 98312 | tf_op jit(solution)/shard_map/ppermute | solution.py:447
  21.7 27.4 %all-to-all-start = ((f32[256,1,128]{2,1,0:T(1,128)}), f32[256,1,128]{2,1,0:T(1,128)S(1)}, u32[]{:S(2)}, u32[]{:S(2)}) async-start(f32[256,1,128]{2,1,0:T(1,128)} %bitcast.3), calls=%async_computation | async-start | bytes 262144 | tf_op jit(solution)/shard_map/all_to_all | solution.py:464
  36.3 3.0 %copy-start.1 = (bf16[4,1568,128]{2,1,0:T(8,128)(2,1)S(1)}, bf16[4,1568,128]{2,1,0:T(8,128)(2,1)}, u32[]{:S(2)}) copy-start(bf16[4,1568,128]{2,1,0:T(8,128)(2,1)} %constant.45.clone.picks_hbm) | copy-start | bytes 4816900
  39.1 9.9 %copy-start.2 = (bf16[63,64,64]{2,1,0:T(8,128)(2,1)S(1)}, bf16[63,64,64]{2,1,0:T(8,128)(2,1)}, u32[]{:S(2)}) copy-start(bf16[63,64,64]{2,1,0:T(8,128)(2,1)} %root_ops.1) | copy-start | bytes 1548292
